TPU v7x, 512 devices: a whole 4x4x16 slice. The times are simulated.
512 devices in a mesh: head: 8 (over y, core), seq: 64 (over x, z).
Axes of the slice: x: 4, y: 4, z: 16, core: 2. Of those that a mesh axis runs over, the one named last changes fastest.
Arguments:
- keys: bfloat16 [1048576, 128], P(('head', 'seq')), parts along dimension 0, may hold values from -6 to 6
- values: bfloat16 [1048576, 128], P(('head', 'seq')), parts along dimension 0, may hold values from -6 to 6
- queries: bfloat16 [1048576, 128], P(('head', 'seq')), parts along dimension 0, may hold values from -160 to 160
- query_positions: int32 [4096], P(('head', 'seq')), parts along dimension 0, may hold values from 0 to 131071, as said below
- kept_index: int32 [4096], P('head'), parts along dimension 0, may hold values from 0 to 131071, as said below
- ridge_level: int32 [8], P('head'), parts along dimension 0, may hold values from 20 to 99
Outputs:
- matched_values: float32 [4096, 128], P('head'), parts along dimension 0
- ref_out: float32 [4096, 128], P(('head', 'seq')), parts along dimension 0
There are 8 independent parts, one for each index of `head`. A program takes and returns all parts, laid end to end along the dimension named above; each array names one. Nothing has to cross between parts.
Inputs may be any that keep to these rules, and one draw needn't show every extreme that they name: `query_positions`: entries 8 d to 8 (d + 1) - 1 are distinct increasing positions within the slab of positions 2048 d to 2048 (d + 1) - 1. `kept_index`: distinct and increasing.
All inputs are finite; a program needn't handle non-finite values.
Results may differ from a plain program's by a relative error of at most 0.00051.
Values may be sent and summed in bfloat16 or wider, within the bound.
No kernel may reach another device: no remote copies, remote signals or barrier semaphores. Data moves between devices by JAX's collectives and lax.ppermute only.
A program may use at most 64 MiB of HBM per device.

v0:
```python
import math

import jax
import jax.numpy as jnp
from jax import lax
from jax.sharding import Mesh
from jax.sharding import PartitionSpec as P

SEQ = ("seq_0", "seq_1")
HEAD_SEQ = ("head", "seq_0", "seq_1")


def joined_along(blocks, dim):
    shape = list(blocks.shape[1:])
    shape[dim] *= blocks.shape[0]
    return jnp.moveaxis(blocks, 0, dim).reshape(shape)


def from_everyone(x, axis):
    size = lax.axis_size(axis)
    return lax.all_to_all(jnp.broadcast_to(x[None], (size, *x.shape)), axis, 0, 0, tiled=True)


def gather_directly(x, axis, dim):
    return joined_along(from_everyone(x, axis), dim)


def split_up(x, dim, size):
    before, after = (x.shape[:dim], x.shape[dim + 1 :])
    return jnp.moveaxis(x.reshape(*before, size, -1, *after), dim, 0)


def summed_on_arrival(x, axis, dim):
    blocks = split_up(x, dim, lax.axis_size(axis))
    arrived = lax.all_to_all(blocks, axis, split_axis=0, concat_axis=0, tiled=True)
    return arrived.sum(axis=0)


def filled_up(lines, size):
    spare = -lines.shape[0] % size
    if not spare:
        return lines
    return jnp.concatenate([lines, jnp.zeros((spare, *lines.shape[1:]), lines.dtype)])


def nested_sum(x, axes):
    lines = x.reshape(-1, x.shape[-1])
    own = summed_on_arrival(filled_up(lines, lax.axis_size(axes)), axes, 0)
    whole = gather_directly(own, axes, 0)
    return whole[: len(lines)].reshape(x.shape)


def gathered_once(x, axis):
    leaves = jax.tree.leaves(x)
    order = sorted(range(len(leaves)), key=lambda k: -leaves[k].size)
    width = (1, *leaves[order[0]].shape)[-1]
    lines = [
        jnp.pad(leaves[k].reshape(-1), (0, -leaves[k].size % width)).reshape(-1, width)
        for k in order
    ]
    both, at, found = (lax.all_gather(jnp.concatenate(lines), axis), 0, {})
    for k, line in zip(order, lines):
        piece = both[:, at : at + len(line)].reshape(len(both), -1)
        found[k] = piece[:, : leaves[k].size].reshape(-1, *leaves[k].shape)
        at += len(line)
    numbers = iter(range(len(leaves)))
    return jax.tree.map(lambda _: found[next(numbers)], x)


def joined_all(x, axes, combine):
    for axis in axes:
        pieces = gathered_once(x, axis)
        x = jax.tree.map(lambda part: part[0], pieces)
        for k in range(1, lax.axis_size(axis)):
            x = combine(x, jax.tree.map(lambda part: part[k], pieces))
    return x


def combine_partials(earlier, later):
    peak_a, total_a, numer_a = earlier
    peak_b, total_b, numer_b = later
    joined = jnp.maximum(peak_a, peak_b)
    factor_a = jnp.exp(peak_a - joined)
    factor_b = jnp.exp(peak_b - joined)
    return (
        joined,
        total_a * factor_a + total_b * factor_b,
        numer_a * factor_a[:, None] + numer_b * factor_b[:, None],
    )


def per_device(keys, values, queries, query_positions, kept_index, ridge_level):
    slab_len = keys.shape[0]
    head_dim = keys.shape[1]
    own_count = query_positions.shape[0]
    inv_root = 1.0 / math.sqrt(head_dim)
    slab_start = lax.axis_index(SEQ) * slab_len
    local_rows = query_positions - slab_start
    own_queries = jnp.take(queries, local_rows, axis=0)
    all_queries = gather_directly(own_queries, SEQ, 0)
    offset = kept_index - slab_start
    inside = ((offset >= 0) & (offset < slab_len)).astype(jnp.float32)
    picked = (
        jnp.take(keys, jnp.clip(offset, 0, slab_len - 1), axis=0).astype(jnp.float32)
        * inside[:, None]
    )
    kept_keys = nested_sum(picked, SEQ).astype(jnp.bfloat16)
    full_logits = jnp.dot(all_queries, kept_keys.T, preferred_element_type=jnp.float32) * inv_root
    weights = jax.nn.softmax(full_logits, axis=1)
    gram_local = jnp.dot(weights.T, weights, precision=lax.Precision.HIGHEST)
    row_count = all_queries.shape[0]
    row_block = math.gcd(row_count, 512)

    def block_partials(query_block):
        scores = jnp.dot(query_block, keys.T, preferred_element_type=jnp.float32) * inv_root
        row_peak = jnp.max(scores, axis=1)
        probs = jnp.exp(scores - row_peak[:, None]).astype(jnp.bfloat16)
        totals = jnp.sum(probs.astype(jnp.float32), axis=1)
        numer = jnp.dot(probs, values, preferred_element_type=jnp.float32)
        return (row_peak, totals, numer)

    peaks, totals, numers = lax.map(
        block_partials, all_queries.reshape(row_count // row_block, row_block, head_dim)
    )
    peaks = peaks.reshape(row_count)
    totals = totals.reshape(row_count)
    numers = numers.reshape(row_count, head_dim)
    own_start = lax.axis_index(SEQ) * own_count
    merged_peak, merged_total, merged_numer = joined_all(
        (peaks, totals, numers), SEQ, combine_partials
    )
    full_ref = merged_numer / merged_total[:, None]
    ref_out = lax.dynamic_slice_in_dim(full_ref, own_start, own_count, 0)
    moment = jnp.dot(weights.T, full_ref, precision=lax.Precision.HIGHEST)
    ridge_value = ridge_level[0].astype(jnp.float32) * 0.01
    system = gram_local + ridge_value * jnp.eye(gram_local.shape[0], dtype=jnp.float32)
    lower = jnp.linalg.cholesky(system)
    matched_values = jax.scipy.linalg.cho_solve((lower, True), moment)
    return (matched_values, ref_out)


def solution(mesh):
    torus = Mesh(mesh.devices.reshape(mesh.shape["head"], 4, 16), ("head", "seq_0", "seq_1"))
    return jax.shard_map(
        per_device,
        mesh=torus,
        in_specs=(
            P(HEAD_SEQ, None),
            P(HEAD_SEQ, None),
            P(HEAD_SEQ, None),
            P(HEAD_SEQ),
            P("head"),
            P("head"),
        ),
        out_specs=(P("head", None), P(HEAD_SEQ, None)),
        check_vma=False,
    )
```

profile of v0, /device:TPU:24, one launch (start us, length us, event | category | flops | bytes accessed | tf_op | source)
XLA Modules:
  0.0 298.7 jit_solution(16105829078610560343)
XLA Ops:
  8.0 1.7 gather_fusion
  9.7 34.7 %all_to_all.15 = bf16[64,8,128]{2,1,0:T(8,128)(2,1)S(1)} all-to-all(bf16[64,8,128]{2,1,0:T(8,128)(2,1)S(1)} %broadcast_in_dim.44), channel_id=1, replica_groups=mesh['head'=8,'seq_0'=4,'seq_1'=16] {'seq_0','seq_1'}, dimensions={0} | all-to-all | bytes 262144 | tf_op jit(solution)/shard_map/all_to_all | solution.py:21
  45.2 0.9 convert_reduce_fusion
  47.8 23.0 %all-gather.5.cloned.1.call-done = f32[2080,128]{1,0:T(8,128)} async-done(((f32[520,128]{1,0:T(8,128)}), f32[2080,128]{1,0:T(8,128)}) %all-gather.5.cloned.1.call-update) | async-done | bytes 1064976 | tf_op jit(solution)/shard_map/all_gather | solution.py:61
  71.4 0.8 fusion.160
  72.9 1.7 fusion.55
  75.4 1.3 gather_fusion.1
  77.1 37.6 %all_to_all.16 = f32[64,8,128]{2,1,0:T(8,128)S(1)} all-to-all(f32[64,8,128]{2,1,0:T(8,128)S(1)} %convert_multiply_fusion), channel_id=1, replica_groups=mesh['head'=8,'seq_0'=4,'seq_1'=16] {'seq_0','seq_1'}, dimensions={0} | all-to-all | bytes 524288 | tf_op jit(solution)/shard_map/all_to_all | solution.py:35
  115.5 6.5 %all-to-all-start.2 = ((bf16[64,8,128]{2,1,0:T(8,128)(2,1)}), bf16[64,8,128]{2,1,0:T(8,128)(2,1)S(1)}, u32[]{:S(2)}, u32[]{:S(2)}) async-start(bf16[64,8,128]{2,1,0:T(8,128)(2,1)} %broadcast_in_dim.49), calls=%async_computation.2 | async-start | bytes 262144 | tf_op jit(solution)/shard_map/all_to_all | solution.py:21
  122.6 15.5 %all-to-all-done.2 = bf16[64,8,128]{2,1,0:T(8,128)(2,1)S(1)} async-done(((bf16[64,8,128]{2,1,0:T(8,128)(2,1)}), bf16[64,8,128]{2,1,0:T(8,128)(2,1)S(1)}, u32[]{:S(2)}, u32[]{:S(2)}) %all-to-all-start.2) | async-done | bytes 131104 | tf_op jit(solution)/shard_map/all_to_all | solution.py:21
  139.4 2.1 fusion.6
  142.1 1.0 copy-done.2
  143.1 11.7 %cholesky.103 = f32[128,128]{1,0:T(8,128)S(1)} custom-call(f32[128,128]{1,0:T(8,128)S(1)} %cholesky.263), custom_call_target="Cholesky" | custom-call | tf_op jit(solution)/shard_map/jit(cholesky)/cholesky | solution.py:137
  155.0 9.8 %custom-call.34 = f32[1,128,128]{1,2,0:T(8,128)S(1)} custom-call(f32[1,128,128]{2,1,0:T(8,128)S(1)} %get-tuple-element.103), custom_call_target="InvertDiagBlocksLowerTriangular" | custom-call | tf_op jit(solution)/shard_map/jit(cholesky)/cholesky | solution.py:137
  164.8 1.2 constant_dynamic-update-slice_fusion.3
  166.0 1.3 convolution_subtract_fusion
  167.3 11.9 %cholesky.215 = f32[128,128]{1,0:T(8,128)S(1)} custom-call(f32[128,128]{1,0:T(8,128)S(1)} %cholesky.267), custom_call_target="Cholesky" | custom-call | tf_op jit(solution)/shard_map/jit(cholesky)/cholesky | solution.py:137
  179.3 9.8 %custom-call.35 = f32[1,128,128]{1,2,0:T(8,128)S(1)} custom-call(f32[1,128,128]{2,1,0:T(8,128)S(1)} %get-tuple-element.100), custom_call_target="InvertDiagBlocksLowerTriangular" | custom-call | tf_op jit(solution)/shard_map/jit(cholesky)/cholesky | solution.py:137
  189.3 1.3 convolution_subtract_fusion.1
  190.6 11.7 %cholesky.236 = f32[128,128]{1,0:T(8,128)S(1)} custom-call(f32[128,128]{1,0:T(8,128)S(1)} %cholesky.272), custom_call_target="Cholesky" | custom-call | tf_op jit(solution)/shard_map/jit(cholesky)/cholesky | solution.py:137
  202.4 9.8 %custom-call.36 = f32[1,128,128]{1,2,0:T(8,128)S(1)} custom-call(f32[1,128,128]{2,1,0:T(8,128)S(1)} %get-tuple-element.97), custom_call_target="InvertDiagBlocksLowerTriangular" | custom-call | tf_op jit(solution)/shard_map/jit(cholesky)/cholesky | solution.py:137
  212.4 1.2 convolution_subtract_fusion.8
  213.7 11.9 %cholesky.253 = f32[128,128]{1,0:T(8,128)S(1)} custom-call(f32[128,128]{1,0:T(8,128)S(1)} %convolution_subtract_fusion.8), custom_call_target="Cholesky" | custom-call | tf_op jit(solution)/shard_map/jit(cholesky)/cholesky | solution.py:137
  230.3 7.9 %while.1 = (s32[]{:T(128)}, f32[512,512]{1,0:T(8,128)S(1)}, s32[4,2]{0,1:T(2,128)S(1)}, f32[4,128,128]{2,1,0:T(8,128)S(1)}, s32[]{:T(128)}) while((s32[]{:T(128)}, f32[512,512]{1,0:T(8,128)S(1)}, s32[4,2]{0,1:T(2,128)S(1)}, f32[4,128,128]{2,1,0:T(8,128)S(1)}, s32[]{:T(128)}) %tuple.81), condition=%wide.while_cond, body=%wide.while_body.sunk | while | flops 2 | bytes 131181 | solution.py:138
  230.9 1.3 bitcast_dynamic-update-slice_fusion.2
  232.9 1.3 bitcast_dynamic-update-slice_fusion.2
  234.9 1.3 bitcast_dynamic-update-slice_fusion.2
  236.9 1.3 bitcast_dynamic-update-slice_fusion.2
  238.2 39.3 %custom-call.37 = f32[4,128,128]{1,2,0:T(8,128)S(1)} custom-call(f32[4,128,128]{2,1,0:T(8,128)S(1)} %get-tuple-element.30), custom_call_target="InvertDiagBlocksLowerTriangular" | custom-call | tf_op jit(solution)/shard_map/jit(_cho_solve)/triangular_solve | solution.py:138
  278.3 1.0 fusion.115
  279.3 4.5 %fusion.10 = f32[512,128]{1,0:T(8,128)S(1)} fusion(f32[16,520,128]{2,1,0:T(8,128)} %bitcast.732, f32[512]{0:T(512)S(1)} %get-tuple-element.39, f32[512]{0:T(512)S(1)} %get-tuple-element.69, f32[512]{0:T(512)S(1)} %get-tuple-element.68, f32[512]{0:T(512)S(1)} %get-tuple-element.67, f32[512]{0:T(512)S(1)} %get-tuple-element.66, f32[512]{0:T(512)S(1)} %get-tuple-element.65, ...), kind=kLoop, calls=%fused_computation.36 | loop fusion | flops 3014656 | bytes 4519936 | tf_op jit(solution)/shard_map/div | solution.py:132
  283.8 2.3 fusion.4
  (77 shorter events, 19.7 us)
Async XLA Ops:
  7.2 37.3 %copy-start = (bf16[2048,128]{1,0:T(8,128)(2,1)S(1)}, bf16[2048,128]{1,0:T(8,128)(2,1)}, u32[]{:S(2)}) copy-start(bf16[2048,128]{1,0:T(8,128)(2,1)} %param.6) | copy-start | bytes 1572868
  7.2 63.6 %all-gather.5.cloned.1.call-start = ((), (), s32[]{:S(2)}) async-start(), calls=%async_computation.3 | async-start | bytes 1331200 | tf_op jit(solution)/shard_map/all_gather | solution.py:61
  45.2 1.0 copy-start.3
  46.1 29.2 %copy-start.4 = (s32[512]{0:T(512)S(1)}, s32[512]{0:T(512)}, u32[]{:S(2)}) copy-start(s32[512]{0:T(512)} %param.10) | copy-start | bytes 6148
  47.7 229.8 %all-gather.7.cloned.1.call-start = ((), (), s32[]{:S(2)}) async-start(), calls=%async_computation.4 | async-start | bytes 4526080 | tf_op jit(solution)/shard_map/all_gather | solution.py:61
  115.5 22.7 %all-to-all-start.2 = ((bf16[64,8,128]{2,1,0:T(8,128)(2,1)}), bf16[64,8,128]{2,1,0:T(8,128)(2,1)S(1)}, u32[]{:S(2)}, u32[]{:S(2)}) async-start(bf16[64,8,128]{2,1,0:T(8,128)(2,1)} %broadcast_in_dim.49), calls=%async_computation.2 | async-start | bytes 262144 | tf_op jit(solution)/shard_map/all_to_all | solution.py:21
  138.5 1.0 copy-start.1
  142.1 1.0 copy-start.2
Sparse Core Ops, SparseCore 0:
  47.9 22.8 all-gather.4
  75.5 91.9 all-gather.6
where the time goes:
time: 305 us; the launch traced here: 299 us
  other arithmetic  133 us (44%)
  blocking collectives  72.3 us (24%)
  waiting for transfers between devices  38.5 us (13%)
  between operations  18.1 us (6%)
  matrix products  15.5 us (5%)
  local copies, waits for them, and re-layouts  14.7 us (5%)
  starting transfers between devices  6.58 us (2%)
    another operation x14, other arithmetic, per_device(): lower = jnp.linalg.cholesky(system)  78.8 us
    another operation x4, other arithmetic, per_device(): matched_values = jax.scipy.linalg.cho_solve((lower, True), moment)  40.2 us
    all_to_all x1, blocking collectives, summed_on_arrival(): lax.all_to_all(blocks, axis, split_axis=0, concat_axis=0, tiled=True)  37.6 us
    all_to_all x1, blocking collectives, from_everyone(): lax.all_to_all(jnp.broadcast_to(x[None], (size, *x.shape)), axis, 0, 0, t...  34.7 us
    all_gather x2, waiting for transfers between devices, gathered_once(): both, at, found = (lax.all_gather(jnp.concatenate(lines), axis), 0, {})  23 us
    all_to_all x1, waiting for transfers between devices, from_everyone(): lax.all_to_all(jnp.broadcast_to(x[None], (size, *x.shape)), axis, 0, 0, t...  15.5 us
    another operation x12, local copies, waits for them, and re-layouts  7.84 us
    all_to_all x1, starting transfers between devices, from_everyone(): lax.all_to_all(jnp.broadcast_to(x[None], (size, *x.shape)), axis, 0, 0, t...  6.5 us
  transfers between devices with their start and end apart: 3, of which 2 were waited for; matrix products, arithmetic and copies ran while one was open for 46% of the time, Pallas kernels for 0%

commit v1 on v0

v1 whole, which is shorter than its diff:
```python
import math

import jax
import jax.numpy as jnp
from jax import lax
from jax.experimental import pallas as pl
from jax.experimental.pallas import tpu as pltpu
from jax.sharding import PartitionSpec as P

SEQ = "seq"
FULL = 32767.0
FINE = 65536.0
LOWEST = -28


def swap(blocks):
    return lax.all_to_all(blocks, SEQ, 0, 0, tiled=True)


def power_of_two(k):
    low = jnp.left_shift(jnp.int32(1), jnp.clip(k + 30, 0, 30)).astype(jnp.float32)
    high = jnp.left_shift(jnp.int32(1), jnp.clip(k, 0, 30)).astype(jnp.float32)
    deep = jnp.left_shift(jnp.int32(1), jnp.clip(k + 60, 0, 30)).astype(jnp.float32)
    return low * (2.0**-30) * high * deep * (2.0**-30)


def code_of(x):
    x = x.astype(jnp.float32)
    size = jnp.abs(x)
    step = jnp.zeros(x.shape, jnp.int32)
    unit = jnp.full(x.shape, 2.0 ** (7 - LOWEST), jnp.float32)
    for e in range(LOWEST + 1, 3):
        reached = size >= 2.0**e
        step = jnp.where(reached, e - LOWEST, step)
        unit = jnp.where(reached, 2.0 ** (7 - e), unit)
    digits = (size * unit).astype(jnp.int32)
    code = jnp.where(size >= 2.0**LOWEST, step * 128 + digits, 0)
    return jnp.where(x < 0, -code, code).astype(jnp.int16)


def decoded(code):
    code = code.astype(jnp.int32)
    size = jnp.maximum(jnp.abs(code) - 128, 0)
    step = size >> 7
    digits = jnp.where(code == 0, 0, (size & 127) + 128)
    value = digits.astype(jnp.float32) * jnp.left_shift(jnp.int32(1), step).astype(jnp.float32)
    value = value * 2.0 ** (LOWEST - 7)
    return jnp.where(code < 0, -value, value).astype(jnp.bfloat16)


def in_two(x):
    high = x.astype(jnp.bfloat16)
    return high, (x - high.astype(jnp.float32)).astype(jnp.bfloat16)


def product(a, b, dims):
    def one(u, v):
        return lax.dot_general(u, v, (dims, ((), ())), preferred_element_type=jnp.float32)

    return one(a[0], b[0]) + (one(a[0], b[1]) + one(a[1], b[0]))


ROWS = ((1,), (0,))
BY_ROW = ((0,), (0,))
BY_COLUMN = ((1,), (1,))


def solve_kernel(level_ref, queries_ref, kept_ref, out_ref, system_ref, weights_ref, inverse_ref, rest_ref):
    size = system_ref.shape[0]
    inv_root = 1.0 / math.sqrt(queries_ref.shape[1])
    logits = lax.dot_general(
        queries_ref[...], kept_ref[...], (BY_COLUMN, ((), ())), preferred_element_type=jnp.float32
    ) * inv_root
    weights = jnp.exp(logits - jnp.max(logits, axis=1, keepdims=True))
    weights = weights / jnp.sum(weights, axis=1, keepdims=True)
    weights_ref[...] = weights
    parts = in_two(weights)
    gram = product(parts, parts, BY_ROW)
    ridge = level_ref[0].astype(jnp.float32) * 0.01
    bound = jnp.max(jnp.sum(weights, axis=0, keepdims=True), axis=1, keepdims=True) * 1.0001
    row = lax.broadcasted_iota(jnp.int32, (size, size), 0)
    column = lax.broadcasted_iota(jnp.int32, (size, size), 1)
    eye = jnp.where(row == column, 1.0, 0.0)
    system = gram + ridge * eye
    system_ref[...] = system
    span = jnp.max(bound) + 2.0 * ridge
    first = 2.0 / span
    rest = eye - first * system
    rest_ref[...] = rest
    inverse_ref[...] = first * eye
    reach = span / jnp.max(bound)

    def step(reach):
        ahead = 2.0 * reach * reach
        scale = ahead / (ahead - 1.0)
        rest = in_two(rest_ref[...])
        inverse = inverse_ref[...]
        inverse_ref[...] = scale * (inverse + product(in_two(inverse), rest, ROWS))
        rest_ref[...] = scale * product(rest, rest, ROWS) - (scale - 1.0) * eye
        return ahead - 1.0

    lax.while_loop(lambda reach: reach < 4096.0, step, reach)
    inverse = inverse_ref[...]
    rest = eye - jnp.dot(
        system_ref[...], inverse, precision=lax.Precision.HIGHEST, preferred_element_type=jnp.float32
    )
    inverse = inverse + product(in_two(inverse), in_two(rest), ROWS)
    out_ref[...] = product(in_two(inverse), in_two(weights_ref[...]), BY_COLUMN)


def solve_rows(level, queries, kept):
    count, size = queries.shape[0], kept.shape[0]
    vmem = pl.BlockSpec(memory_space=pltpu.VMEM)
    return pl.pallas_call(
        solve_kernel,
        out_shape=jax.ShapeDtypeStruct((size, count), jnp.float32),
        in_specs=[pl.BlockSpec(memory_space=pltpu.SMEM), vmem, vmem],
        out_specs=vmem,
        scratch_shapes=[
            pltpu.VMEM((size, size), jnp.float32),
            pltpu.VMEM((count, size), jnp.float32),
            pltpu.VMEM((size, size), jnp.float32),
            pltpu.VMEM((size, size), jnp.float32),
        ],
        compiler_params=pltpu.CompilerParams(vmem_limit_bytes=40 * 2**20),
        cost_estimate=pl.CostEstimate(flops=12 * 10**9, bytes_accessed=2 * 2**20, transcendentals=2**18),
        name="solve",
    )(level, queries, kept)


def per_device(keys, values, queries, query_positions, kept_index, ridge_level):
    slab_len, head_dim = keys.shape
    own_count = query_positions.shape[0]
    peers = lax.axis_size(SEQ)
    own_kept = kept_index.shape[0] // peers
    inv_root = 1.0 / math.sqrt(head_dim)
    slab_start = lax.axis_index(SEQ) * slab_len
    own_queries = jnp.take(queries, query_positions - slab_start, axis=0)
    offset = kept_index - slab_start
    inside = (offset >= 0) & (offset < slab_len)
    picked = jnp.where(
        inside[:, None], jnp.take(keys, jnp.clip(offset, 0, slab_len - 1), axis=0), 0
    ).astype(jnp.bfloat16)
    sent = jnp.concatenate(
        [
            jnp.broadcast_to(own_queries[None], (peers, own_count, head_dim)),
            picked.reshape(peers, own_kept, head_dim),
        ],
        axis=1,
    )
    got = swap(sent)
    all_queries = got[:, :own_count].reshape(peers * own_count, head_dim)
    kept_block = jnp.sum(got[:, own_count:].astype(jnp.float32), axis=0)

    scores = jnp.dot(all_queries, keys.T, preferred_element_type=jnp.float32) * inv_root
    peak = jnp.max(scores, axis=1)
    probs = jnp.exp(scores - peak[:, None]).astype(jnp.bfloat16)
    total = jnp.sum(probs.astype(jnp.float32), axis=1)
    numer = jnp.dot(probs, values, preferred_element_type=jnp.float32)

    mean = numer / total[:, None]
    most = jnp.max(jnp.abs(mean), axis=1)
    power = jnp.clip(jnp.ceil(jnp.log2(jnp.maximum(most, 2.0**-58))), -58, 3).astype(jnp.int32)
    spread = mean / power_of_two(power)[:, None]
    coarse = jnp.clip(jnp.round(spread * FULL), -FULL, FULL).astype(jnp.int16)

    def in_words(x):
        whole = jnp.floor(x)
        fine = jnp.minimum(jnp.round((x - whole) * FINE), FINE - 1.0) - FINE / 2
        return whole, fine

    peak_whole, peak_fine = in_words(peak)
    sent_peak = peak_whole + (peak_fine + FINE / 2) / FINE
    share_whole, share_fine = in_words(jnp.log(total) + (peak - sent_peak))
    marks = jnp.stack([peak_whole, peak_fine, share_whole, share_fine, power.astype(jnp.float32)], axis=-1)
    marks = jnp.pad(marks, ((0, 0), (0, head_dim - marks.shape[1]))).astype(jnp.int16)
    sent = jnp.concatenate(
        [
            coarse.reshape(peers, own_count, head_dim),
            jnp.broadcast_to(code_of(kept_block)[None], (peers, own_kept, head_dim)),
            marks.reshape(peers, own_count, head_dim),
        ],
        axis=1,
    )
    got = swap(sent)
    kept_keys = decoded(got[:, own_count : own_count + own_kept]).reshape(peers * own_kept, head_dim)
    marks = got[:, own_count + own_kept :].astype(jnp.float32)
    peaks = marks[:, :, 0] + (marks[:, :, 1] + FINE / 2) / FINE
    shares = marks[:, :, 2] + (marks[:, :, 3] + FINE / 2) / FINE
    factors = jnp.exp(peaks - jnp.max(peaks, axis=0)[None] + shares)
    scales = factors * power_of_two(marks[:, :, 4].astype(jnp.int32)) / FULL
    means = got[:, :own_count].astype(jnp.float32)
    ref_out = jnp.sum(means * scales[:, :, None], axis=0) / jnp.sum(factors, axis=0)[:, None]

    whole = swap(jnp.broadcast_to(ref_out[None], (peers, own_count, head_dim)))
    rows = solve_rows(ridge_level, all_queries, kept_keys)
    whole = whole.reshape(peers * own_count, head_dim)
    matched_values = jnp.dot(rows, whole, precision=lax.Precision.HIGHEST)
    return (matched_values, ref_out)


def solution(mesh):
    return jax.shard_map(
        per_device,
        mesh=mesh,
        in_specs=(
            P(("head", "seq"), None),
            P(("head", "seq"), None),
            P(("head", "seq"), None),
            P(("head", "seq")),
            P("head"),
            P("head"),
        ),
        out_specs=(P("head", None), P(("head", "seq"), None)),
        check_vma=False,
    )
```

time: 305 us -> 112 us (0.37); the launches traced: 299 us -> 111 us
  other arithmetic: 133 us -> 4.51 us
  blocking collectives: 72.3 us -> 39.3 us
  between operations: 18.1 us -> 1.48 us
  Pallas kernels: 0 us -> 12.6 us
  matrix products: 15.5 us -> 3.27 us
  local copies, waits for them, and re-layouts: 14.7 us -> 4.95 us
  starting transfers between devices: 6.58 us -> 13.3 us
  waiting for transfers between devices: 38.5 us -> 31.9 us
    another operation x18 -> x3, other arithmetic: 119 us -> 0.06 us  [the longest x14 78.8 us: per_device(): lower = jnp.linalg.cholesky(system)]
    all_to_all x2 -> x1, blocking collectives: 72.3 us -> 39.3 us  [swap(): return lax.all_to_all(blocks, SEQ, 0, 0, tiled=True)]
    all_gather x2 -> x0, waiting for transfers between devices: 23 us -> none  [gathered_once(): both, at, found = (lax.all_gather(jnp.concatenate(lines), axis), 0, {})]
    all_to_all x1 -> x2, waiting for transfers between devices: 15.5 us -> 31.9 us  [swap(): return lax.all_to_all(blocks, SEQ, 0, 0, tiled=True)]
    pallas_call x0 -> x1, Pallas kernels: none -> 12.6 us  [solve_rows(): pl.pallas_call(solve_kernel, out_shape=jax.ShapeDtypeStruct((size, count)...]
    another operation x20 -> x0, matrix products: 9.38 us -> none  [the longest x6 5.47 us: per_device(): lower = jnp.linalg.cholesky(system)]
    another operation x17 -> x2, local copies, waits for them, and re-layouts: 7.99 us -> 0.04 us  [the longest x1 0.04 us: per_device(): jnp.stack([peak_whole, peak_fine, share_whole, share_fine, power.astype(j...]
    all_to_all x1 -> x2, starting transfers between devices: 6.5 us -> 13.3 us  [swap(): return lax.all_to_all(blocks, SEQ, 0, 0, tiled=True)]
  transfers between devices with their start and end apart: 3 -> 2, of which waited for: 2 -> 2; matrix products, arithmetic and copies ran while one was open for 46% -> 0% of each run, Pallas kernels for 0% -> 11%
where the time goes in v1:
time: 112 us; the launch traced here: 111 us
  blocking collectives  39.3 us (35%)
  waiting for transfers between devices  31.9 us (28%)
  starting transfers between devices  13.3 us (12%)
  Pallas kernels  12.6 us (11%)
  local copies, waits for them, and re-layouts  4.95 us (4%)
  other arithmetic  4.51 us (4%)
  matrix products  3.27 us (3%)
  between operations  1.48 us (1%)
    all_to_all x1, blocking collectives, swap(): return lax.all_to_all(blocks, SEQ, 0, 0, tiled=True)  39.3 us
    all_to_all x2, waiting for transfers between devices, swap(): return lax.all_to_all(blocks, SEQ, 0, 0, tiled=True)  31.9 us
    all_to_all x2, starting transfers between devices, swap(): return lax.all_to_all(blocks, SEQ, 0, 0, tiled=True)  13.3 us
    pallas_call x1, Pallas kernels, solve_rows(): pl.pallas_call(solve_kernel, out_shape=jax.ShapeDtypeStruct((size, count)...  12.6 us
  transfers between devices with their start and end apart: 2, of which 2 were waited for; matrix products, arithmetic and copies ran while one was open for 0% of the time, Pallas kernels for 11%

profile of v1, /device:TPU:24, one launch (start us, length us, event | category | flops | bytes accessed | tf_op | source)
XLA Modules:
  0.0 111.4 jit_solution(2301523023534370576)
XLA Ops:
  0.6 0.7 compare_and_fusion
  1.4 0.1 broadcast_in_dim.261
  1.5 0.1 broadcast_in_dim.263
  1.6 0.7 compare_and_fusion.2
  2.3 1.3 %gather_fusion.1 = bf16[512,128]{1,0:T(8,128)(2,1)S(1)} fusion(bf16[2048,128]{1,0:T(8,128)(2,1)S(1)} %copy-done, s32[1024]{0:T(1024)S(1)} %pad_clamp_fusion), kind=kCustom, calls=%fused_computation.1 | custom fusion | bytes 264192 | tf_op jit(solution)/shard_map/jit(_take)/gather | solution.py:142
  3.6 1.7 %gather_fusion = bf16[8,128]{1,0:T(8,128)(2,1)S(1)} fusion(bf16[2048,128]{1,0:T(8,128)(2,1)} %param.8, s32[1024]{0:T(1024)S(1)} %pad_clamp_fusion.1), kind=kCustom, calls=%fused_computation | custom fusion | bytes 4128 | tf_op jit(solution)/shard_map/jit(_take)/gather | solution.py:138
  5.3 0.1 broadcast_select_fusion
  5.4 0.2 fusion.15
  5.7 39.3 %all_to_all.15 = bf16[64,16,128]{2,1,0:T(8,128)(2,1)S(1)} all-to-all(bf16[64,16,128]{2,1,0:T(8,128)(2,1)S(1)} %pad_maximum_fusion), channel_id=1, replica_groups=mesh['head'=8,'seq'=64] {'seq'}, dimensions={0} | all-to-all | bytes 524288 | tf_op jit(solution)/shard_map/all_to_all | solution.py:17
  45.0 0.8 multiply_reduce_fusion
  45.8 0.9 convert_reduce_fusion
  46.7 0.1 copy-done.2
  46.9 0.8 abs_reduce_fusion
  47.8 0.2 copy.41
  48.0 0.1 convert_reduce_fusion.1
  48.1 0.1 fusion.16
  48.3 0.8 pad_add_fusion
  49.1 6.4 %all-to-all-start.1 = ((s16[64,24,128]{2,1,0:T(8,128)(2,1)}), s16[64,24,128]{2,1,0:T(8,128)(2,1)S(1)}, u32[]{:S(2)}, u32[]{:S(2)}) async-start(s16[64,24,128]{2,1,0:T(8,128)(2,1)} %pad_add_fusion), calls=%async_computation.1 | async-start | bytes 786432 | tf_op jit(solution)/shard_map/all_to_all | solution.py:17
  56.2 24.7 %all-to-all-done.1 = s16[64,24,128]{2,1,0:T(8,128)(2,1)S(1)} async-done(((s16[64,24,128]{2,1,0:T(8,128)(2,1)}), s16[64,24,128]{2,1,0:T(8,128)(2,1)S(1)}, u32[]{:S(2)}, u32[]{:S(2)}) %all-to-all-start.1) | async-done | bytes 393248 | tf_op jit(solution)/shard_map/all_to_all | solution.py:17
  81.0 0.3 copy.40
  81.3 0.1 convert_element_type.132
  81.3 0.1 fusion.29
  81.5 0.2 fusion.23
  81.6 0.1 multiply_bitcast_fusion
  81.7 0.1 copy.35
  81.8 0.3 multiply_reduce_fusion.1
  82.1 0.1 copy.39
  82.3 0.7 broadcast_in_dim.331
  83.0 6.8 %all-to-all-start.2 = ((f32[64,8,128]{2,1,0:T(8,128)}), f32[64,8,128]{2,1,0:T(8,128)S(1)}, u32[]{:S(2)}, u32[]{:S(2)}) async-start(f32[64,8,128]{2,1,0:T(8,128)} %broadcast_in_dim.331), calls=%async_computation.2 | async-start | bytes 524288 | tf_op jit(solution)/shard_map/all_to_all | solution.py:17
  89.8 12.6 %solve.1 = f32[512,512]{1,0:T(8,128)S(1)} custom-call(s32[1]{0:T(128)S(6)} %copy.42.level_ref, bf16[512,128]{1,0:T(8,128)(2,1)S(1)} %slice_bitcast_fusion.queries_ref, bf16[512,128]{1,0:T(8,128)(2,1)S(1)} %get-tuple-element.13.kept_ref), custom_call_target="tpu_custom_call" | custom-call | flops 12000000000 | bytes 2097152 | tf_op jit(solution)/shard_map/solve/pallas_call | solution.py:114
  102.5 7.2 %all-to-all-done.2 = f32[64,8,128]{2,1,0:T(8,128)S(1)} async-done(((f32[64,8,128]{2,1,0:T(8,128)}), f32[64,8,128]{2,1,0:T(8,128)S(1)}, u32[]{:S(2)}, u32[]{:S(2)}) %all-to-all-start.2) | async-done | bytes 262176 | tf_op jit(solution)/shard_map/all_to_all | solution.py:17
  109.7 1.7 %fusion.11 = f32[512,128]{1,0:T(8,128)} fusion(f32[512,512]{1,0:T(8,128)S(1)} %solve.1, f32[64,8,128]{2,1,0:T(8,128)S(1)} %all-to-all-done.2), kind=kOutput, calls=%fused_computation.22 | convolution fusion | flops 402653184 | bytes 1572864 | tf_op jit(solution)/shard_map/dot_general | solution.py:198
  (21 shorter events, 0.4 us)
Async XLA Ops:
  0.6 1.7 %copy-start = (bf16[2048,128]{1,0:T(8,128)(2,1)S(1)}, bf16[2048,128]{1,0:T(8,128)(2,1)}, u32[]{:S(2)}) copy-start(bf16[2048,128]{1,0:T(8,128)(2,1)} %param.6) | copy-start | bytes 1572868
  45.8 1.0 copy-start.2
  49.1 31.8 %all-to-all-start.1 = ((s16[64,24,128]{2,1,0:T(8,128)(2,1)}), s16[64,24,128]{2,1,0:T(8,128)(2,1)S(1)}, u32[]{:S(2)}, u32[]{:S(2)}) async-start(s16[64,24,128]{2,1,0:T(8,128)(2,1)} %pad_add_fusion), calls=%async_computation.1 | async-start | bytes 786432 | tf_op jit(solution)/shard_map/all_to_all | solution.py:17
  82.3 20.2 %copy-start.1 = (f32[8,128]{1,0:T(8,128)}, f32[8,128]{1,0:T(8,128)S(1)}, u32[]{:S(2)}) copy-start(f32[8,128]{1,0:T(8,128)S(1)} %copy.37) | copy-start | bytes 12292
  83.0 26.7 %all-to-all-start.2 = ((f32[64,8,128]{2,1,0:T(8,128)}), f32[64,8,128]{2,1,0:T(8,128)S(1)}, u32[]{:S(2)}, u32[]{:S(2)}) async-start(f32[64,8,128]{2,1,0:T(8,128)} %broadcast_in_dim.331), calls=%async_computation.2 | async-start | bytes 524288 | tf_op jit(solution)/shard_map/all_to_all | solution.py:17

commit v2 on v1

--- a/solution.py
+++ b/solution.py
@@ -1,3 +1,4 @@
+import functools
 import math
 
 import jax
@@ -15,13 +16,6 @@
 
 def swap(blocks):
     return lax.all_to_all(blocks, SEQ, 0, 0, tiled=True)
-
-
-def power_of_two(k):
-    low = jnp.left_shift(jnp.int32(1), jnp.clip(k + 30, 0, 30)).astype(jnp.float32)
-    high = jnp.left_shift(jnp.int32(1), jnp.clip(k, 0, 30)).astype(jnp.float32)
-    deep = jnp.left_shift(jnp.int32(1), jnp.clip(k + 60, 0, 30)).astype(jnp.float32)
-    return low * (2.0**-30) * high * deep * (2.0**-30)
 
 
 def code_of(x):
@@ -35,7 +29,7 @@
         unit = jnp.where(reached, 2.0 ** (7 - e), unit)
     digits = (size * unit).astype(jnp.int32)
     code = jnp.where(size >= 2.0**LOWEST, step * 128 + digits, 0)
-    return jnp.where(x < 0, -code, code).astype(jnp.int16)
+    return jnp.where(x < 0, -code, code).astype(jnp.float32)
 
 
 def decoded(code):
@@ -128,74 +122,140 @@
     )(level, queries, kept)
 
 
+def pick_kernel(start_ref, positions_ref, kept_ref, keys_ref, queries_ref, out_ref):
+    slab_len, head_dim = keys_ref.shape
+    peers = out_ref.shape[0]
+    own_count = positions_ref.shape[0]
+    start = start_ref[0]
+    lane = lax.broadcasted_iota(jnp.int32, (1, head_dim), 1)
+
+    def one_hot(places):
+        return jnp.concatenate(
+            [
+                jnp.where(places == (lane + at).astype(jnp.float32), 1.0, 0.0).astype(jnp.bfloat16)
+                for at in range(0, slab_len, head_dim)
+            ],
+            axis=1,
+        )
+
+    offset = (kept_ref[...] - start).astype(jnp.float32)
+    offset = jnp.transpose(jnp.broadcast_to(offset, (head_dim, offset.shape[1])))
+    picked = jnp.dot(one_hot(offset), keys_ref[...], preferred_element_type=jnp.float32)
+    row = lax.broadcasted_iota(jnp.int32, (2 * own_count, head_dim), 0)
+    place = jnp.full((2 * own_count, head_dim), -1, jnp.int32)
+    for k in range(own_count):
+        place = jnp.where(row == k, positions_ref[k] - start, place)
+    own = jnp.dot(one_hot(place.astype(jnp.float32)), queries_ref[...], preferred_element_type=jnp.float32)
+    own = jnp.broadcast_to(own[None, :own_count], (peers, own_count, head_dim))
+    picked = picked.reshape(peers, -1, head_dim)
+    out_ref[...] = jnp.concatenate([own, picked], axis=1).astype(jnp.bfloat16)
+
+
+def in_words(x):
+    whole = jnp.floor(x)
+    fine = jnp.minimum(jnp.round((x - whole) * FINE), FINE - 1.0) - FINE / 2
+    return whole, fine
+
+
+def power_of_two(k):
+    return jnp.exp(k * math.log(2.0))
+
+
+def attend_kernel(own_count, got_ref, keys_ref, values_ref, queries_ref, coarse_ref, marks_ref, code_ref):
+    head_dim = keys_ref.shape[1]
+    peers = got_ref.shape[0]
+    rows = peers * own_count
+    inv_root = 1.0 / math.sqrt(head_dim)
+    got = got_ref[...].astype(jnp.float32)
+    code_ref[...] = code_of(jnp.sum(got[:, own_count:], axis=0))
+    queries_ref[...] = got[:, :own_count].reshape(rows, head_dim).astype(jnp.bfloat16)
+    block = rows // 2
+    for at in range(0, rows, block):
+        scores = lax.dot_general(
+            queries_ref[at : at + block], keys_ref[...], (BY_COLUMN, ((), ())), preferred_element_type=jnp.float32
+        ) * inv_root
+        peak = jnp.max(scores, axis=1, keepdims=True)
+        probs = jnp.exp(scores - peak).astype(jnp.bfloat16)
+        total = jnp.sum(probs.astype(jnp.float32), axis=1, keepdims=True)
+        mean = jnp.dot(probs, values_ref[...], preferred_element_type=jnp.float32) / total
+        most = jnp.max(jnp.abs(mean), axis=1, keepdims=True)
+        power = jnp.ceil(jnp.log(jnp.maximum(most, 2.0**-58)) / math.log(2.0))
+        coarse_ref[at : at + block] = jnp.clip(jnp.round(mean / power_of_two(power) * FULL), -FULL, FULL)
+        peak_whole, peak_fine = in_words(peak)
+        sent_peak = peak_whole + (peak_fine + FINE / 2) / FINE
+        share_whole, share_fine = in_words(jnp.log(total) + (peak - sent_peak))
+        lane = lax.broadcasted_iota(jnp.int32, (block, head_dim), 1)
+        row = lax.broadcasted_iota(jnp.int32, (block, head_dim), 0)
+        place = lane - (row & (own_count - 1))
+        marks = jnp.zeros((block, head_dim), jnp.float32)
+        for k, mark in enumerate((peak_whole, peak_fine, share_whole, share_fine, power)):
+            marks = jnp.where(place == k * own_count, mark, marks)
+        marks = jnp.sum(marks.reshape(block // own_count, own_count, head_dim), axis=1)
+        marks_ref[at // own_count : (at + block) // own_count] = marks
+
+
 def per_device(keys, values, queries, query_positions, kept_index, ridge_level):
     slab_len, head_dim = keys.shape
     own_count = query_positions.shape[0]
     peers = lax.axis_size(SEQ)
     own_kept = kept_index.shape[0] // peers
-    inv_root = 1.0 / math.sqrt(head_dim)
-    slab_start = lax.axis_index(SEQ) * slab_len
-    own_queries = jnp.take(queries, query_positions - slab_start, axis=0)
-    offset = kept_index - slab_start
-    inside = (offset >= 0) & (offset < slab_len)
-    picked = jnp.where(
-        inside[:, None], jnp.take(keys, jnp.clip(offset, 0, slab_len - 1), axis=0), 0
-    ).astype(jnp.bfloat16)
+    vmem = pl.BlockSpec(memory_space=pltpu.VMEM)
+    smem = pl.BlockSpec(memory_space=pltpu.SMEM)
+    roomy = pltpu.CompilerParams(vmem_limit_bytes=40 * 2**20)
+    slab_start = (lax.axis_index(SEQ) * slab_len).astype(jnp.int32).reshape(1)
+    sent = pl.pallas_call(
+        pick_kernel,
+        out_shape=jax.ShapeDtypeStruct((peers, own_count + own_kept, head_dim), jnp.bfloat16),
+        in_specs=[smem, smem, vmem, vmem, vmem],
+        out_specs=vmem,
+        compiler_params=roomy,
+        name="pick",
+    )(slab_start, query_positions, kept_index[None], keys, queries)
+    got = swap(sent)
+    rows = peers * own_count
+    all_queries, coarse, marks, code = pl.pallas_call(
+        functools.partial(attend_kernel, own_count),
+        out_shape=[
+            jax.ShapeDtypeStruct((rows, head_dim), jnp.bfloat16),
+            jax.ShapeDtypeStruct((rows, head_dim), jnp.float32),
+            jax.ShapeDtypeStruct((peers, head_dim), jnp.float32),
+            jax.ShapeDtypeStruct((own_kept, head_dim), jnp.float32),
+        ],
+        in_specs=[vmem] * 3,
+        out_specs=[vmem] * 4,
+        compiler_params=roomy,
+        name="attend",
+    )(got, keys, values)
     sent = jnp.concatenate(
         [
-            jnp.broadcast_to(own_queries[None], (peers, own_count, head_dim)),
-            picked.reshape(peers, own_kept, head_dim),
+            coarse.reshape(peers, own_count // 2, 2, head_dim),
+            jnp.broadcast_to(code.reshape(own_kept // 2, 2, head_dim), (peers, own_kept // 2, 2, head_dim)),
+            jnp.pad(marks.reshape(peers, 1, 1, head_dim), ((0, 0), (0, 0), (0, 1), (0, 0))),
         ],
         axis=1,
-    )
+    ).astype(jnp.int16)
     got = swap(sent)
-    all_queries = got[:, :own_count].reshape(peers * own_count, head_dim)
-    kept_block = jnp.sum(got[:, own_count:].astype(jnp.float32), axis=0)
-
-    scores = jnp.dot(all_queries, keys.T, preferred_element_type=jnp.float32) * inv_root
-    peak = jnp.max(scores, axis=1)
-    probs = jnp.exp(scores - peak[:, None]).astype(jnp.bfloat16)
-    total = jnp.sum(probs.astype(jnp.float32), axis=1)
-    numer = jnp.dot(probs, values, preferred_element_type=jnp.float32)
-
-    mean = numer / total[:, None]
-    most = jnp.max(jnp.abs(mean), axis=1)
-    power = jnp.clip(jnp.ceil(jnp.log2(jnp.maximum(most, 2.0**-58))), -58, 3).astype(jnp.int32)
-    spread = mean / power_of_two(power)[:, None]
-    coarse = jnp.clip(jnp.round(spread * FULL), -FULL, FULL).astype(jnp.int16)
-
-    def in_words(x):
-        whole = jnp.floor(x)
-        fine = jnp.minimum(jnp.round((x - whole) * FINE), FINE - 1.0) - FINE / 2
-        return whole, fine
-
-    peak_whole, peak_fine = in_words(peak)
-    sent_peak = peak_whole + (peak_fine + FINE / 2) / FINE
-    share_whole, share_fine = in_words(jnp.log(total) + (peak - sent_peak))
-    marks = jnp.stack([peak_whole, peak_fine, share_whole, share_fine, power.astype(jnp.float32)], axis=-1)
-    marks = jnp.pad(marks, ((0, 0), (0, head_dim - marks.shape[1]))).astype(jnp.int16)
-    sent = jnp.concatenate(
-        [
-            coarse.reshape(peers, own_count, head_dim),
-            jnp.broadcast_to(code_of(kept_block)[None], (peers, own_kept, head_dim)),
-            marks.reshape(peers, own_count, head_dim),
-        ],
-        axis=1,
-    )
-    got = swap(sent)
-    kept_keys = decoded(got[:, own_count : own_count + own_kept]).reshape(peers * own_kept, head_dim)
-    marks = got[:, own_count + own_kept :].astype(jnp.float32)
-    peaks = marks[:, :, 0] + (marks[:, :, 1] + FINE / 2) / FINE
-    shares = marks[:, :, 2] + (marks[:, :, 3] + FINE / 2) / FINE
+    kept_keys = decoded(got[:, own_count // 2 : (own_count + own_kept) // 2]).reshape(peers * own_kept, head_dim)
+    marks = got[:, -1, 0].astype(jnp.float32)
+    marks = [marks[:, k * own_count : (k + 1) * own_count] for k in range(5)]
+    peaks = marks[0] + (marks[1] + FINE / 2) / FINE
+    shares = marks[2] + (marks[3] + FINE / 2) / FINE
     factors = jnp.exp(peaks - jnp.max(peaks, axis=0)[None] + shares)
-    scales = factors * power_of_two(marks[:, :, 4].astype(jnp.int32)) / FULL
-    means = got[:, :own_count].astype(jnp.float32)
-    ref_out = jnp.sum(means * scales[:, :, None], axis=0) / jnp.sum(factors, axis=0)[:, None]
-
-    whole = swap(jnp.broadcast_to(ref_out[None], (peers, own_count, head_dim)))
-    rows = solve_rows(ridge_level, all_queries, kept_keys)
-    whole = whole.reshape(peers * own_count, head_dim)
-    matched_values = jnp.dot(rows, whole, precision=lax.Precision.HIGHEST)
+    scales = factors * power_of_two(marks[4]) / FULL / jnp.sum(factors, axis=0)[None]
+    means = got[:, : own_count // 2].reshape(peers, own_count, head_dim).astype(jnp.float32)
+    ref_out = jnp.sum(means * scales[:, :, None], axis=0)
+
+    most = jnp.max(jnp.abs(ref_out), axis=1, keepdims=True)
+    power = jnp.ceil(jnp.log(jnp.maximum(most, 2.0**-58)) / math.log(2.0))
+    coarse = jnp.clip(jnp.round(ref_out / power_of_two(power) * FULL), -FULL, FULL)
+    power = jnp.pad(power.reshape(1, own_count), ((0, 1), (0, head_dim - own_count)))
+    sent = jnp.concatenate([coarse, power], axis=0).reshape(1, own_count // 2 + 1, 2, head_dim).astype(jnp.int16)
+    whole = swap(jnp.broadcast_to(sent, (peers, *sent.shape[1:])))
+    answer = solve_rows(ridge_level, all_queries, kept_keys)
+    power = whole[:, -1, 0, :own_count].astype(jnp.float32)
+    whole = whole[:, :-1].reshape(peers, own_count, head_dim).astype(jnp.float32)
+    whole = (whole * (power_of_two(power) / FULL)[:, :, None]).reshape(rows, head_dim)
+    matched_values = jnp.dot(answer, whole, precision=lax.Precision.HIGH)
     return (matched_values, ref_out)
 
 

time: 112 us -> 104 us (0.929)
  waiting for transfers between devices: 31.9 us -> 22.5 us
  Pallas kernels: 12.6 us -> 18.3 us
  matrix products: 3.27 us -> 1.38 us
  other arithmetic: 4.51 us -> 2.72 us
    all_to_all x2, waiting for transfers between devices: 31.9 us -> 22.5 us  [swap(): return lax.all_to_all(blocks, SEQ, 0, 0, tiled=True)]
    pallas_call x0 -> x2, Pallas kernels: none -> 3.85 us  [the longest x1 2.48 us: per_device(): pl.pallas_call(functools.partial(attend_kernel, own_count), out_shape=[ja...]
    gather x2 -> x0, local copies, waits for them, and re-layouts: 3.01 us -> none  [the longest x1 1.67 us: per_device(): own_queries = jnp.take(queries, query_positions - slab_start, axis=0)]
    unnamed x9 -> x17, local copies, waits for them, and re-layouts: 0.74 us -> 3.3 us
    dot_general x3 -> x1, matrix products: 3.27 us -> 1.38 us  [per_device(): matched_values = jnp.dot(answer, whole, precision=lax.Precision.HIGH)]
    pallas_call x1, Pallas kernels: 12.6 us -> 14.4 us  [solve_rows(): pl.pallas_call(solve_kernel, out_shape=jax.ShapeDtypeStruct((size, count)...]
    and x2 -> x0, other arithmetic: 1.42 us -> none  [the longest x1 0.75 us: per_device(): jnp.take(keys, jnp.clip(offset, 0, slab_len - 1), axis=0)]
  transfers between devices with their start and end apart: 2 -> 2, of which waited for: 2 -> 2; matrix products, arithmetic and copies ran while one was open for 0% -> 0% of each run, Pallas kernels for 11% -> 14%
where the time goes in v2:
time: 104 us
  blocking collectives  39.5 us (38%)
  waiting for transfers between devices  22.5 us (22%)
  Pallas kernels  18.3 us (18%)
  starting transfers between devices  13 us (12%)
  local copies, waits for them, and re-layouts  4.8 us (5%)
  other arithmetic  2.72 us (3%)
  between operations  1.44 us (1%)
  matrix products  1.38 us (1%)
    all_to_all x1, blocking collectives, swap(): return lax.all_to_all(blocks, SEQ, 0, 0, tiled=True)  39.5 us
    all_to_all x2, waiting for transfers between devices, swap(): return lax.all_to_all(blocks, SEQ, 0, 0, tiled=True)  22.5 us
    pallas_call x1, Pallas kernels, solve_rows(): pl.pallas_call(solve_kernel, out_shape=jax.ShapeDtypeStruct((size, count)...  14.4 us
    all_to_all x2, starting transfers between devices, swap(): return lax.all_to_all(blocks, SEQ, 0, 0, tiled=True)  13 us
    unnamed x17, local copies, waits for them, and re-layouts  3.3 us
    pallas_call x1, Pallas kernels, per_device(): pl.pallas_call(functools.partial(attend_kernel, own_count), out_shape=[ja...  2.48 us
  transfers between devices with their start and end apart: 2, of which 2 were waited for; matrix products, arithmetic and copies ran while one was open for 0% of the time, Pallas kernels for 14%

profile of v2, /device:TPU:24, one launch (start us, length us, event | category | flops | bytes accessed | tf_op | source)
XLA Modules:
  0.0 103.7 jit_solution(15717620791564663678)
XLA Ops:
  0.7 0.7 copy-done.4
  1.3 1.0 %copy-done = bf16[2048,128]{1,0:T(8,128)(2,1)S(1)} copy-done((bf16[2048,128]{1,0:T(8,128)(2,1)S(1)}, bf16[2048,128]{1,0:T(8,128)(2,1)}, u32[]{:S(2)}) %copy-start) | copy-done | bytes 524312
  2.4 1.0 %copy-done.2 = bf16[2048,128]{1,0:T(8,128)(2,1)S(1)} copy-done((bf16[2048,128]{1,0:T(8,128)(2,1)S(1)}, bf16[2048,128]{1,0:T(8,128)(2,1)}, u32[]{:S(2)}) %copy-start.2) | copy-done | bytes 524312
  3.4 1.4 %pick.1 = bf16[64,16,128]{2,1,0:T(8,128)(2,1)S(1)} custom-call(s32[1]{0:T(128)} %bitcast.start_ref, s32[8]{0:T(128)S(1)} %copy-done.5, s32[1,512]{1,0:T(1,128)S(1)} %bitcast.20, bf16[2048,128]{1,0:T(8,128)(2,1)S(1)} %copy-done, bf16[2048,128]{1,0:T(8,128)(2,1)S(1)} %copy-done.2), custom_call_target="tpu_custom_call" | custom-call | tf_op jit(solution)/shard_map/pick/pallas_call | solution.py:206
  4.8 39.5 %all_to_all.15.got_ref = bf16[64,16,128]{2,1,0:T(8,128)(2,1)S(1)} all-to-all(bf16[64,16,128]{2,1,0:T(8,128)(2,1)S(1)} %pick.1), channel_id=1, replica_groups=mesh['head'=8,'seq'=64] {'seq'}, dimensions={0} | all-to-all | bytes 524288 | tf_op jit(solution)/shard_map/all_to_all | solution.py:18
  44.3 2.5 %attend.1 = (bf16[512,128]{1,0:T(8,128)(2,1)S(1)}, f32[512,128]{1,0:T(8,128)S(1)}, f32[64,128]{1,0:T(8,128)S(1)}, f32[8,128]{1,0:T(8,128)S(1)}) custom-call(bf16[64,16,128]{2,1,0:T(8,128)(2,1)S(1)} %all_to_all.15.got_ref, bf16[2048,128]{1,0:T(8,128)(2,1)S(1)} %copy-done.1, bf16[2048,128]{1,0:T(8,128)(2,1)S(1)} %copy-done.3), custom_call_target="tpu_custom_call" | custom-call | tf_op jit(solution)/shard_map/attend/pallas_call | solution.py:216
  46.8 0.1 convert.25
  46.9 0.1 broadcast_in_dim.9
  47.0 1.0 pad_add_fusion
  48.0 6.4 %all-to-all-start.1 = ((s16[64,9,2,128]{3,2,1,0:T(2,128)(2,1)}), s16[64,9,2,128]{3,2,1,0:T(2,128)(2,1)S(1)}, u32[]{:S(2)}, u32[]{:S(2)}) async-start(s16[64,9,2,128]{3,2,1,0:T(2,128)(2,1)} %pad_add_fusion), calls=%async_computation.1 | async-start | bytes 589824 | tf_op jit(solution)/shard_map/all_to_all | solution.py:18
  55.1 20.8 %all-to-all-done.1 = s16[64,9,2,128]{3,2,1,0:T(2,128)(2,1)S(1)} async-done(((s16[64,9,2,128]{3,2,1,0:T(2,128)(2,1)}), s16[64,9,2,128]{3,2,1,0:T(2,128)(2,1)S(1)}, u32[]{:S(2)}, u32[]{:S(2)}) %all-to-all-start.1) | async-done | bytes 294944 | tf_op jit(solution)/shard_map/all_to_all | solution.py:18
  75.9 0.1 copy.24
  76.1 0.1 fusion.19
  76.2 0.2 fusion.20
  76.4 0.1 fusion.11
  76.5 0.1 copy.21
  76.6 1.1 %multiply_reduce_fusion = (f32[4,2,128]{2,1,0:T(2,128)S(1)}, bf16[64,4,2,128]{3,2,1,0:T(2,128)(2,1)S(1)}) fusion(s16[64,9,2,128]{3,2,1,0:T(2,128)(2,1)S(1)} %all-to-all-done.1, f32[64,4,2]{2,1,0:T(4,128)S(1)} %copy.21), kind=kLoop, calls=%fused_computation.12 | loop fusion | flops 1375232 | bytes 399360 | tf_op jit(solution)/shard_map/reduce_sum | solution.py:246
  77.7 0.0 copy-start.6
  77.7 0.1 abs_reduce_fusion
  77.8 0.1 ceil.24
  77.9 0.1 reshape.123
  78.0 0.3 copy-done.6
  78.3 0.1 clamp_convert_fusion
  78.4 0.8 broadcast_in_dim.10
  79.2 6.6 %all-to-all-start.2 = ((s16[64,5,2,128]{3,2,1,0:T(2,128)(2,1)}), s16[64,5,2,128]{3,2,1,0:T(2,128)(2,1)S(1)}, u32[]{:S(2)}, u32[]{:S(2)}) async-start(s16[64,5,2,128]{3,2,1,0:T(2,128)(2,1)} %broadcast_in_dim.10), calls=%async_computation.2 | async-start | bytes 327680 | tf_op jit(solution)/shard_map/all_to_all | solution.py:18
  85.8 14.4 %solve.1 = f32[512,512]{1,0:T(8,128)S(1)} custom-call(s32[1]{0:T(128)S(6)} %copy.27.level_ref, bf16[512,128]{1,0:T(8,128)(2,1)S(1)} %get-tuple-element.6.queries_ref, bf16[512,128]{1,0:T(8,128)(2,1)S(1)} %bitcast.19), custom_call_target="tpu_custom_call" | custom-call | flops 12000000000 | bytes 2097152 | tf_op jit(solution)/shard_map/solve/pallas_call | solution.py:108
  100.2 1.7 %all-to-all-done.2 = s16[64,5,2,128]{3,2,1,0:T(2,128)(2,1)S(1)} async-done(((s16[64,5,2,128]{3,2,1,0:T(2,128)(2,1)}), s16[64,5,2,128]{3,2,1,0:T(2,128)(2,1)S(1)}, u32[]{:S(2)}, u32[]{:S(2)}) %all-to-all-start.2) | async-done | bytes 163872 | tf_op jit(solution)/shard_map/all_to_all | solution.py:18
  101.9 0.1 copy.25
  102.0 0.1 copy.23
  102.1 0.1 div.42
  102.2 0.1 slice.48
  102.3 1.4 %fusion.6 = f32[512,128]{1,0:T(8,128)} fusion(f32[512,512]{1,0:T(8,128)S(1)} %solve.1, s16[512,128]{1,0:T(8,128)(2,1)S(1)} %bitcast.22, f32[512]{0:T(512)S(1)} %div.42), kind=kOutput, calls=%fused_computation.11 | convolution fusion | flops 201457664 | bytes 1443840 | tf_op jit(solution)/shard_map/dot_general | solution.py:258
  (19 shorter events, 0.2 us)
Async XLA Ops:
  0.6 0.7 copy-start.4
  0.6 0.7 copy-start.5
  1.3 1.0 %copy-start = (bf16[2048,128]{1,0:T(8,128)(2,1)S(1)}, bf16[2048,128]{1,0:T(8,128)(2,1)}, u32[]{:S(2)}) copy-start(bf16[2048,128]{1,0:T(8,128)(2,1)} %keys_ref.3) | copy-start | bytes 1572868
  2.4 1.0 %copy-start.2 = (bf16[2048,128]{1,0:T(8,128)(2,1)S(1)}, bf16[2048,128]{1,0:T(8,128)(2,1)}, u32[]{:S(2)}) copy-start(bf16[2048,128]{1,0:T(8,128)(2,1)} %queries_ref.1) | copy-start | bytes 1572868
  3.4 40.9 %copy-start.3 = (bf16[2048,128]{1,0:T(8,128)(2,1)S(1)}, bf16[2048,128]{1,0:T(8,128)(2,1)}, u32[]{:S(2)}) copy-start(bf16[2048,128]{1,0:T(8,128)(2,1)} %values_ref.1) | copy-start | bytes 1572868
  4.8 39.5 %copy-start.1 = (bf16[2048,128]{1,0:T(8,128)(2,1)S(1)}, bf16[2048,128]{1,0:T(8,128)(2,1)}, u32[]{:S(2)}) copy-start(bf16[2048,128]{1,0:T(8,128)(2,1)} %keys_ref.3) | copy-start | bytes 1572868
  48.0 28.0 %all-to-all-start.1 = ((s16[64,9,2,128]{3,2,1,0:T(2,128)(2,1)}), s16[64,9,2,128]{3,2,1,0:T(2,128)(2,1)S(1)}, u32[]{:S(2)}, u32[]{:S(2)}) async-start(s16[64,9,2,128]{3,2,1,0:T(2,128)(2,1)} %pad_add_fusion), calls=%async_computation.1 | async-start | bytes 589824 | tf_op jit(solution)/shard_map/all_to_all | solution.py:18
  77.7 0.6 copy-start.6
  79.2 22.7 %all-to-all-start.2 = ((s16[64,5,2,128]{3,2,1,0:T(2,128)(2,1)}), s16[64,5,2,128]{3,2,1,0:T(2,128)(2,1)S(1)}, u32[]{:S(2)}, u32[]{:S(2)}) async-start(s16[64,5,2,128]{3,2,1,0:T(2,128)(2,1)} %broadcast_in_dim.10), calls=%async_computation.2 | async-start | bytes 327680 | tf_op jit(solution)/shard_map/all_to_all | solution.py:18

commit v3 on v2

v3 whole, which is shorter than its diff:
```python
import functools
import math

import jax
import jax.numpy as jnp
from jax import lax
from jax.experimental import pallas as pl
from jax.experimental.pallas import tpu as pltpu
from jax.sharding import PartitionSpec as P

SEQ = "seq"
FULL = 32767.0
PEAK_UNIT = 2.0**17
SHARE_UNIT = 2.0**26
LANES = 128
TILE = 16
KEY_PARTS = 4
LOWEST = -28


def swap(blocks):
    return lax.all_to_all(blocks, SEQ, 0, 0, tiled=True)


def code_of(x):
    x = x.astype(jnp.float32)
    size = jnp.abs(x)
    step = jnp.zeros(x.shape, jnp.int32)
    unit = jnp.full(x.shape, 2.0 ** (7 - LOWEST), jnp.float32)
    for e in range(LOWEST + 1, 3):
        reached = size >= 2.0**e
        step = jnp.where(reached, e - LOWEST, step)
        unit = jnp.where(reached, 2.0 ** (7 - e), unit)
    digits = (size * unit).astype(jnp.int32)
    code = jnp.where(size >= 2.0**LOWEST, step * 128 + digits, 0)
    return jnp.where(x < 0, -code, code)


def decoded(code):
    size = jnp.maximum(jnp.abs(code) - 128, 0)
    step = size >> 7
    digits = jnp.where(code == 0, 0, (size & 127) + 128)
    value = digits.astype(jnp.float32) * jnp.left_shift(jnp.int32(1), step).astype(jnp.float32)
    value = value * 2.0 ** (LOWEST - 7)
    return jnp.where(code < 0, -value, value)


def packed(high, low):
    return (high << 16) | (low & 0xFFFF)


def high_of(word):
    return word >> 16


def low_of(word):
    return (word << 16) >> 16


def every(ref, first, stride):
    return ref[pl.ds(first, ref.shape[0] // stride, stride=stride)]


def power_of_two(k):
    return jnp.exp(k * math.log(2.0))


def scaled(x):
    most = jnp.max(jnp.abs(x), axis=1, keepdims=True)
    power = jnp.ceil(jnp.log(jnp.maximum(most, 2.0**-58)) / math.log(2.0))
    whole = jnp.clip(jnp.round(x / power_of_two(power) * FULL), -FULL, FULL)
    return whole.astype(jnp.int32), power


def in_lanes(columns, own_count):
    rows = columns[0].shape[0]
    lane = lax.broadcasted_iota(jnp.int32, (rows, LANES), 1)
    row = lax.broadcasted_iota(jnp.int32, (rows, LANES), 0)
    place = lane - (row & (own_count - 1))
    marks = jnp.zeros((rows, LANES), jnp.float32)
    for k, column in enumerate(columns):
        marks = jnp.where(place == k * own_count, column, marks)
    return jnp.sum(marks.reshape(rows // own_count, own_count, LANES), axis=1)


def in_two(x):
    high = x.astype(jnp.bfloat16)
    return high, (x - high.astype(jnp.float32)).astype(jnp.bfloat16)


def product(a, b, dims):
    def one(u, v):
        return lax.dot_general(u, v, (dims, ((), ())), preferred_element_type=jnp.float32)

    return one(a[0], b[0]) + (one(a[0], b[1]) + one(a[1], b[0]))


ROWS = ((1,), (0,))
BY_ROW = ((0,), (0,))
BY_COLUMN = ((1,), (1,))


def solve_kernel(own_count, level_ref, queries_ref, words_ref, high_ref, low_ref, kept_ref, system_ref, weights_ref, inverse_ref, rest_ref):
    size = system_ref.shape[0]
    inv_root = 1.0 / math.sqrt(queries_ref.shape[1])
    for k in range(own_count):
        kept_ref[pl.ds(k, size // own_count, stride=own_count)] = decoded(low_of(every(words_ref, k, own_count + 1)))
    kept = kept_ref[...].astype(jnp.bfloat16)
    logits = lax.dot_general(
        queries_ref[...], kept, (BY_COLUMN, ((), ())), preferred_element_type=jnp.float32
    ) * inv_root
    weights = jnp.exp(logits - jnp.max(logits, axis=1, keepdims=True))
    weights = weights / jnp.sum(weights, axis=1, keepdims=True)
    weights_ref[...] = weights
    parts = in_two(weights)
    gram = product(parts, parts, BY_ROW)
    ridge = level_ref[0].astype(jnp.float32) * 0.01
    bound = jnp.max(jnp.sum(weights, axis=0, keepdims=True), axis=1, keepdims=True) * 1.0001
    row = lax.broadcasted_iota(jnp.int32, (size, size), 0)
    column = lax.broadcasted_iota(jnp.int32, (size, size), 1)
    eye = jnp.where(row == column, 1.0, 0.0)
    system = gram + ridge * eye
    system_ref[...] = system
    span = jnp.max(bound) + 2.0 * ridge
    first = 2.0 / span
    rest = eye - first * system
    rest_ref[...] = rest
    inverse_ref[...] = first * eye
    reach = span / jnp.max(bound)

    def step(reach):
        ahead = 2.0 * reach * reach
        scale = ahead / (ahead - 1.0)
        rest = in_two(rest_ref[...])
        inverse = inverse_ref[...]
        inverse_ref[...] = scale * (inverse + product(in_two(inverse), rest, ROWS))
        rest_ref[...] = scale * product(rest, rest, ROWS) - (scale - 1.0) * eye
        return ahead - 1.0

    lax.while_loop(lambda reach: reach < 4096.0, step, reach)
    inverse = inverse_ref[...]
    rest = eye - jnp.dot(
        system_ref[...], inverse, precision=lax.Precision.HIGHEST, preferred_element_type=jnp.float32
    )
    inverse = inverse + product(in_two(inverse), in_two(rest), ROWS)
    high_ref[...], low_ref[...] = in_two(product(in_two(inverse), in_two(weights_ref[...]), BY_COLUMN))


def pick_kernel(start_ref, positions_ref, kept_hbm, keys_hbm, queries_hbm, out_ref, kept_ref, keys_ref, near_ref, sems, near_sems):
    slab_len = keys_ref.shape[0]
    peers = out_ref.shape[0]
    own_count = positions_ref.shape[0]
    start = start_ref[0]
    tile = near_ref.shape[0] // own_count
    rest = keys_ref.shape[0] // KEY_PARTS
    copies = [pltpu.make_async_copy(kept_hbm, kept_ref, sems.at[KEY_PARTS])]
    for k in range(KEY_PARTS):
        part = pl.ds(k * rest, rest)
        copies.append(pltpu.make_async_copy(keys_hbm.at[part], keys_ref.at[part], sems.at[k]))
    places = [jnp.clip(positions_ref[k] - start, 0, slab_len - 1) for k in range(own_count)]
    near = []
    for k in range(own_count):
        first = pl.multiple_of((places[k] // tile) * tile, tile)
        near.append(pltpu.make_async_copy(queries_hbm.at[pl.ds(first, tile)], near_ref.at[pl.ds(k * tile, tile)], near_sems.at[k]))
    for copy in copies + near:
        copy.start()
    lane = lax.broadcasted_iota(jnp.int32, (1, LANES), 1)

    def one_hot(places, size):
        return jnp.concatenate(
            [
                jnp.where(places == (lane + at).astype(jnp.float32), 1.0, 0.0).astype(jnp.bfloat16)
                for at in range(0, size, LANES)
            ],
            axis=1,
        )

    row = lax.broadcasted_iota(jnp.int32, (2 * own_count, LANES), 0)
    place = jnp.full((2 * own_count, LANES), -1, jnp.int32)
    for k in range(own_count):
        place = jnp.where(row == k, k * tile + places[k] % tile, place)
    copies[0].wait()
    offset = (kept_ref[...] - start).astype(jnp.float32)
    offset = jnp.transpose(jnp.broadcast_to(offset, (LANES, offset.shape[1])))
    chosen = one_hot(offset, slab_len)
    for copy in near:
        copy.wait()
    own = jnp.dot(one_hot(place.astype(jnp.float32), own_count * tile), near_ref[...], preferred_element_type=jnp.float32)
    own = jnp.broadcast_to(own[None, :own_count], (peers, own_count, LANES))
    for copy in copies[1:]:
        copy.wait()
    picked = jnp.dot(chosen, keys_ref[...], preferred_element_type=jnp.float32)
    picked = picked.reshape(peers, -1, LANES)
    out_ref[...] = jnp.concatenate([own, picked], axis=1).astype(jnp.bfloat16)


def attend_kernel(own_count, got_ref, keys_ref, values_ref, queries_ref, out_ref, word_ref, mark_ref):
    peers = got_ref.shape[0]
    rows = peers * own_count
    inv_root = 1.0 / math.sqrt(keys_ref.shape[1])
    got = got_ref[...].astype(jnp.float32)
    code = code_of(jnp.sum(got[:, own_count:], axis=0))
    queries_ref[...] = got[:, :own_count].reshape(rows, LANES).astype(jnp.bfloat16)
    block = rows // 2
    for at in range(0, rows, block):
        scores = lax.dot_general(
            queries_ref[at : at + block], keys_ref[...], (BY_COLUMN, ((), ())), preferred_element_type=jnp.float32
        ) * inv_root
        peak = jnp.max(scores, axis=1, keepdims=True)
        probs = jnp.exp(scores - peak).astype(jnp.bfloat16)
        total = jnp.sum(probs.astype(jnp.float32), axis=1, keepdims=True)
        mean = jnp.dot(probs, values_ref[...], preferred_element_type=jnp.float32) / total
        whole, power = scaled(mean)
        words = packed(whole.reshape(block // own_count, own_count, LANES), code[None])
        word_ref[at : at + block] = words.reshape(block, LANES)
        peak_mark = jnp.round(peak * PEAK_UNIT)
        share_mark = jnp.round((jnp.log(total) + (peak - peak_mark / PEAK_UNIT)) * SHARE_UNIT)
        marks = in_lanes((peak_mark, share_mark, power), own_count)
        mark_ref[at // own_count : (at + block) // own_count] = marks.astype(jnp.int32)
    for k in range(own_count):
        out_ref[pl.ds(k, peers, stride=own_count + 1)] = every(word_ref, k, own_count)
    out_ref[pl.ds(own_count, peers, stride=own_count + 1)] = mark_ref[...]


def merge_kernel(words_ref, ref_out_ref, out_ref):
    own_count = ref_out_ref.shape[0]
    marks = every(words_ref, own_count, own_count + 1).astype(jnp.float32)
    peaks = marks[:, :own_count] / PEAK_UNIT
    shares = marks[:, own_count : 2 * own_count] / SHARE_UNIT
    powers = marks[:, 2 * own_count : 3 * own_count]
    factors = jnp.exp(peaks - jnp.max(peaks, axis=0, keepdims=True) + shares)
    scales = factors * power_of_two(powers) * (1.0 / FULL) / jnp.sum(factors, axis=0, keepdims=True)
    ref_out = jnp.concatenate(
        [
            jnp.sum(
                high_of(every(words_ref, k, own_count + 1)).astype(jnp.float32) * scales[:, k : k + 1],
                axis=0,
                keepdims=True,
            )
            for k in range(own_count)
        ],
        axis=0,
    )
    ref_out_ref[...] = ref_out
    whole, power = scaled(ref_out)
    half = own_count // 2
    words = packed(whole[:half], whole[half:])
    words = jnp.concatenate([words, in_lanes((power,), own_count).astype(jnp.int32)], axis=0)
    peers = out_ref.shape[0] // (half + 1)
    for k in range(half + 1):
        out_ref[pl.ds(k, peers, stride=half + 1)] = jnp.broadcast_to(words[k : k + 1], (peers, LANES))


def finish_kernel(own_count, words_ref, high_ref, low_ref, out_ref, rows_ref):
    half = own_count // 2
    peers = words_ref.shape[0] // (half + 1)
    scales = power_of_two(every(words_ref, half, half + 1).astype(jnp.float32)[:, :own_count]) * (1.0 / FULL)
    for k in range(own_count):
        words = every(words_ref, k % half, half + 1)
        whole = high_of(words) if k < half else low_of(words)
        rows_ref[pl.ds(k, peers, stride=own_count)] = whole.astype(jnp.float32) * scales[:, k : k + 1]
    out_ref[...] = product((high_ref[...], low_ref[...]), in_two(rows_ref[...]), ROWS)


def per_device(keys, values, queries, query_positions, kept_index, ridge_level):
    slab_len, head_dim = keys.shape
    own_count = query_positions.shape[0]
    kept_count = kept_index.shape[0]
    peers = lax.axis_size(SEQ)
    own_kept = kept_count // peers
    rows = peers * own_count
    vmem = pl.BlockSpec(memory_space=pltpu.VMEM)
    smem = pl.BlockSpec(memory_space=pltpu.SMEM)
    hbm = pl.BlockSpec(memory_space=pltpu.HBM)
    roomy = pltpu.CompilerParams(vmem_limit_bytes=24 * 2**20)
    whole = pltpu.CompilerParams(vmem_limit_bytes=60 * 2**20)
    small = pltpu.CompilerParams(vmem_limit_bytes=8 * 2**20)
    f32, bf16, i32 = jnp.float32, jnp.bfloat16, jnp.int32
    slab_start = (lax.axis_index(SEQ) * slab_len).astype(i32).reshape(1)
    sent = pl.pallas_call(
        pick_kernel,
        out_shape=jax.ShapeDtypeStruct((peers, own_count + own_kept, head_dim), bf16),
        in_specs=[smem, smem, hbm, hbm, hbm],
        out_specs=vmem,
        scratch_shapes=[
            pltpu.VMEM((1, kept_count), i32),
            pltpu.VMEM((slab_len, head_dim), bf16),
            pltpu.VMEM((own_count * TILE, head_dim), bf16),
            pltpu.SemaphoreType.DMA((KEY_PARTS + 1,)),
            pltpu.SemaphoreType.DMA((own_count,)),
        ],
        compiler_params=whole,
        name="pick",
    )(slab_start, query_positions, kept_index[None], keys, queries)
    got = swap(sent)
    all_queries, words = pl.pallas_call(
        functools.partial(attend_kernel, own_count),
        out_shape=[
            jax.ShapeDtypeStruct((rows, head_dim), bf16),
            jax.ShapeDtypeStruct((peers * (own_count + 1), LANES), i32),
        ],
        in_specs=[vmem] * 3,
        out_specs=[vmem] * 2,
        scratch_shapes=[pltpu.VMEM((rows, head_dim), i32), pltpu.VMEM((peers, LANES), i32)],
        compiler_params=roomy,
        name="attend",
    )(got, keys, values)
    words = swap(words.reshape(peers, own_count + 1, 1, LANES)).reshape(words.shape)
    ref_out, means = pl.pallas_call(
        merge_kernel,
        out_shape=[
            jax.ShapeDtypeStruct((own_count, head_dim), f32),
            jax.ShapeDtypeStruct((peers * (own_count // 2 + 1), LANES), i32),
        ],
        in_specs=[vmem],
        out_specs=[vmem] * 2,
        compiler_params=small,
        name="merge",
    )(words)
    means = swap(means.reshape(peers, own_count // 2 + 1, 1, LANES)).reshape(means.shape)
    square = (kept_count, kept_count)
    high, low = pl.pallas_call(
        functools.partial(solve_kernel, own_count),
        out_shape=[jax.ShapeDtypeStruct((kept_count, rows), bf16)] * 2,
        in_specs=[smem, vmem, vmem],
        out_specs=[vmem] * 2,
        scratch_shapes=[
            pltpu.VMEM((kept_count, head_dim), f32),
            pltpu.VMEM(square, f32),
            pltpu.VMEM((rows, kept_count), f32),
            pltpu.VMEM(square, f32),
            pltpu.VMEM(square, f32),
        ],
        compiler_params=roomy,
        cost_estimate=pl.CostEstimate(flops=12 * 10**9, bytes_accessed=2 * 2**20, transcendentals=2**18),
        name="solve",
    )(ridge_level, all_queries, words)
    matched_values = pl.pallas_call(
        functools.partial(finish_kernel, own_count),
        out_shape=jax.ShapeDtypeStruct((kept_count, head_dim), f32),
        in_specs=[vmem] * 3,
        out_specs=vmem,
        scratch_shapes=[pltpu.VMEM((rows, head_dim), f32)],
        compiler_params=roomy,
        name="finish",
    )(means, high, low)
    return (matched_values, ref_out)


def solution(mesh):
    return jax.shard_map(
        per_device,
        mesh=mesh,
        in_specs=(
            P(("head", "seq"), None),
            P(("head", "seq"), None),
            P(("head", "seq"), None),
            P(("head", "seq")),
            P("head"),
            P("head"),
        ),
        out_specs=(P("head", None), P(("head", "seq"), None)),
        check_vma=False,
    )
```

time: 104 us -> 101 us (0.971)
  local copies, waits for them, and re-layouts: 4.8 us -> 0.01 us
  Pallas kernels: 18.3 us -> 22 us
  other arithmetic: 2.72 us -> 0 us
  waiting for transfers between devices: 22.5 us -> 24.2 us
  matrix products: 1.38 us -> 0 us
    unnamed x17 -> x4, local copies, waits for them, and re-layouts: 3.3 us -> 0.01 us
    pallas_call x1, Pallas kernels: 1.36 us -> 3.55 us  [per_device(): pl.pallas_call(pick_kernel, out_shape=jax.ShapeDtypeStruct((peers, own_co...]
    all_to_all x2, waiting for transfers between devices: 22.5 us -> 24.2 us  [swap(): return lax.all_to_all(blocks, SEQ, 0, 0, tiled=True)]
    dot_general x1 -> x0, matrix products: 1.38 us -> none  [per_device(): matched_values = jnp.dot(answer, whole, precision=lax.Precision.HIGH)]
    reduce_sum x2 -> x0, other arithmetic: 1.27 us -> none  [the longest x1 1.08 us: per_device(): ref_out = jnp.sum(means * scales[:, :, None], axis=0)]
    pallas_call x1 -> x3, Pallas kernels: 14.4 us -> 15.3 us  [the longest x1 12.8 us: per_device(): pl.pallas_call(functools.partial(solve_kernel, own_count), out_shape=[jax...]
  transfers between devices with their start and end apart: 2 -> 2, of which waited for: 2 -> 2; matrix products, arithmetic and copies ran while one was open for 0% -> 0% of each run, Pallas kernels for 14% -> 13%
where the time goes in v3:
time: 101 us; the launch traced here: 100 us
  blocking collectives  39.7 us (39%)
  waiting for transfers between devices  24.2 us (24%)
  Pallas kernels  22 us (22%)
  starting transfers between devices  13 us (13%)
  between operations  1.33 us (1%)
    all_to_all x1, blocking collectives, swap(): return lax.all_to_all(blocks, SEQ, 0, 0, tiled=True)  39.7 us
    all_to_all x2, waiting for transfers between devices, swap(): return lax.all_to_all(blocks, SEQ, 0, 0, tiled=True)  24.2 us
    all_to_all x2, starting transfers between devices, swap(): return lax.all_to_all(blocks, SEQ, 0, 0, tiled=True)  13 us
    pallas_call x1, Pallas kernels, per_device(): pl.pallas_call(functools.partial(solve_kernel, own_count), out_shape=[jax...  12.8 us
    pallas_call x1, Pallas kernels, per_device(): pl.pallas_call(pick_kernel, out_shape=jax.ShapeDtypeStruct((peers, own_co...  3.55 us
    pallas_call x1, Pallas kernels, per_device(): pl.pallas_call(functools.partial(attend_kernel, own_count), out_shape=[ja...  3.16 us
  transfers between devices with their start and end apart: 2, of which 2 were waited for; matrix products, arithmetic and copies ran while one was open for 0% of the time, Pallas kernels for 13%

profile of v3, /device:TPU:24, one launch (start us, length us, event | category | flops | bytes accessed | tf_op | source)
XLA Modules:
  0.0 100.3 jit_solution(14577694748584864095)
XLA Ops:
  0.6 0.0 copy-start.1
  0.6 3.5 %pick.1 = bf16[64,16,128]{2,1,0:T(8,128)(2,1)} custom-call(s32[1]{0:T(128)} %bitcast.start_ref, s32[8]{0:T(128)} %positions_ref.1, s32[1,512]{1,0:T(1,128)} %bitcast.9, bf16[2048,128]{1,0:T(8,128)(2,1)} %keys_ref.1, bf16[2048,128]{1,0:T(8,128)(2,1)} %queries_hbm.1), custom_call_target="tpu_custom_call" | custom-call | tf_op jit(solution)/shard_map/pick/pallas_call | solution.py:280
  4.2 0.0 copy-start
  4.2 39.7 %all_to_all.15.got_ref = bf16[64,16,128]{2,1,0:T(8,128)(2,1)S(1)} all-to-all(bf16[64,16,128]{2,1,0:T(8,128)(2,1)} %pick.1), channel_id=1, replica_groups=mesh['head'=8,'seq'=64] {'seq'}, dimensions={0} | all-to-all | bytes 524288 | tf_op jit(solution)/shard_map/all_to_all | solution.py:22
  43.9 0.0 copy-done.1
  43.9 0.0 copy-done
  43.9 3.2 %attend.1 = (bf16[512,128]{1,0:T(8,128)(2,1)S(1)}, s32[576,128]{1,0:T(8,128)}) custom-call(bf16[64,16,128]{2,1,0:T(8,128)(2,1)S(1)} %all_to_all.15.got_ref, bf16[2048,128]{1,0:T(8,128)(2,1)S(1)} %copy-done, bf16[2048,128]{1,0:T(8,128)(2,1)S(1)} %copy-done.1), custom_call_target="tpu_custom_call" | custom-call | tf_op jit(solution)/shard_map/attend/pallas_call | solution.py:296
  47.1 6.4 %all-to-all-start.1 = ((s32[64,9,1,128]{3,2,1,0:T(1,128)}), s32[64,9,1,128]{3,2,1,0:T(1,128)S(1)}, u32[]{:S(2)}, u32[]{:S(2)}) async-start(s32[64,9,1,128]{3,2,1,0:T(1,128)} %bitcast.2), calls=%async_computation.1 | async-start | bytes 589824 | tf_op jit(solution)/shard_map/all_to_all | solution.py:22
  54.2 20.9 %all-to-all-done.1 = s32[64,9,1,128]{3,2,1,0:T(1,128)S(1)} async-done(((s32[64,9,1,128]{3,2,1,0:T(1,128)}), s32[64,9,1,128]{3,2,1,0:T(1,128)S(1)}, u32[]{:S(2)}, u32[]{:S(2)}) %all-to-all-start.1) | async-done | bytes 294944 | tf_op jit(solution)/shard_map/all_to_all | solution.py:22
  75.0 1.1 %merge.1 = (f32[8,128]{1,0:T(8,128)}, s32[320,128]{1,0:T(8,128)}) custom-call(s32[576,128]{1,0:T(8,128)S(1)} %bitcast.6), custom_call_target="tpu_custom_call" | custom-call | tf_op jit(solution)/shard_map/merge/pallas_call | solution.py:309
  76.1 6.6 %all-to-all-start.2 = ((s32[64,5,1,128]{3,2,1,0:T(1,128)}), s32[64,5,1,128]{3,2,1,0:T(1,128)S(1)}, u32[]{:S(2)}, u32[]{:S(2)}) async-start(s32[64,5,1,128]{3,2,1,0:T(1,128)} %bitcast.4), calls=%async_computation.2 | async-start | bytes 327680 | tf_op jit(solution)/shard_map/all_to_all | solution.py:22
  82.7 12.8 %solve.1 = (bf16[512,512]{1,0:T(8,128)(2,1)S(1)}, bf16[512,512]{1,0:T(8,128)(2,1)S(1)}) custom-call(s32[1]{0:T(128)S(6)} %copy.10.level_ref, bf16[512,128]{1,0:T(8,128)(2,1)S(1)} %get-tuple-element.10.queries_ref, s32[576,128]{1,0:T(8,128)S(1)} %bitcast.7), custom_call_target="tpu_custom_call" | custom-call | flops 12000000000 | bytes 2097152 | tf_op jit(solution)/shard_map/solve/pallas_call | solution.py:322
  95.5 3.3 %all-to-all-done.2 = s32[64,5,1,128]{3,2,1,0:T(1,128)S(1)} async-done(((s32[64,5,1,128]{3,2,1,0:T(1,128)}), s32[64,5,1,128]{3,2,1,0:T(1,128)S(1)}, u32[]{:S(2)}, u32[]{:S(2)}) %all-to-all-start.2) | async-done | bytes 163872 | tf_op jit(solution)/shard_map/all_to_all | solution.py:22
  98.8 1.5 %finish.1 = f32[512,128]{1,0:T(8,128)} custom-call(s32[320,128]{1,0:T(8,128)S(1)} %bitcast.8, bf16[512,512]{1,0:T(8,128)(2,1)S(1)} %get-tuple-element.11.high_ref, bf16[512,512]{1,0:T(8,128)(2,1)S(1)} %get-tuple-element.12.low_ref), custom_call_target="tpu_custom_call" | custom-call | tf_op jit(solution)/shard_map/finish/pallas_call | solution.py:338
Async XLA Ops:
  0.6 43.3 %copy-start.1 = (bf16[2048,128]{1,0:T(8,128)(2,1)S(1)}, bf16[2048,128]{1,0:T(8,128)(2,1)}, u32[]{:S(2)}) copy-start(bf16[2048,128]{1,0:T(8,128)(2,1)} %values_ref.1) | copy-start | bytes 1572868
  4.2 39.7 %copy-start = (bf16[2048,128]{1,0:T(8,128)(2,1)S(1)}, bf16[2048,128]{1,0:T(8,128)(2,1)}, u32[]{:S(2)}) copy-start(bf16[2048,128]{1,0:T(8,128)(2,1)} %keys_ref.1) | copy-start | bytes 1572868
  47.1 28.0 %all-to-all-start.1 = ((s32[64,9,1,128]{3,2,1,0:T(1,128)}), s32[64,9,1,128]{3,2,1,0:T(1,128)S(1)}, u32[]{:S(2)}, u32[]{:S(2)}) async-start(s32[64,9,1,128]{3,2,1,0:T(1,128)} %bitcast.2), calls=%async_computation.1 | async-start | bytes 589824 | tf_op jit(solution)/shard_map/all_to_all | solution.py:22
  76.1 22.7 %all-to-all-start.2 = ((s32[64,5,1,128]{3,2,1,0:T(1,128)}), s32[64,5,1,128]{3,2,1,0:T(1,128)S(1)}, u32[]{:S(2)}, u32[]{:S(2)}) async-start(s32[64,5,1,128]{3,2,1,0:T(1,128)} %bitcast.4), calls=%async_computation.2 | async-start | bytes 327680 | tf_op jit(solution)/shard_map/all_to_all | solution.py:22

commit v4 on v3

--- a/solution.py
+++ b/solution.py
@@ -146,24 +146,42 @@
     high_ref[...], low_ref[...] = in_two(product(in_two(inverse), in_two(weights_ref[...]), BY_COLUMN))
 
 
-def pick_kernel(start_ref, positions_ref, kept_hbm, keys_hbm, queries_hbm, out_ref, kept_ref, keys_ref, near_ref, sems, near_sems):
+def sent_out(source, target, sems, first, rows, parts=2):
+    size = rows // parts
+    copies = []
+    for k in range(parts):
+        part = pl.ds(first + k * size, size)
+        copies.append(pltpu.make_async_copy(source.at[part], target.at[part], sems.at[k]))
+        copies[-1].start()
+    return copies
+
+
+def pick_kernel(
+    positions_hbm, kept_hbm, keys_hbm, queries_hbm, out_hbm,
+    positions_ref, kept_ref, keys_ref, near_ref, out_ref, first_sems, sems, near_sems, out_sems,
+):
     slab_len = keys_ref.shape[0]
     peers = out_ref.shape[0]
     own_count = positions_ref.shape[0]
-    start = start_ref[0]
+    start = lax.axis_index(SEQ).astype(jnp.int32) * slab_len
     tile = near_ref.shape[0] // own_count
     rest = keys_ref.shape[0] // KEY_PARTS
-    copies = [pltpu.make_async_copy(kept_hbm, kept_ref, sems.at[KEY_PARTS])]
+    positions_copy = pltpu.make_async_copy(positions_hbm, positions_ref, first_sems.at[0])
+    kept_copy = pltpu.make_async_copy(kept_hbm, kept_ref, first_sems.at[1])
+    positions_copy.start()
+    kept_copy.start()
+    copies = []
     for k in range(KEY_PARTS):
         part = pl.ds(k * rest, rest)
         copies.append(pltpu.make_async_copy(keys_hbm.at[part], keys_ref.at[part], sems.at[k]))
+        copies[-1].start()
+    positions_copy.wait()
     places = [jnp.clip(positions_ref[k] - start, 0, slab_len - 1) for k in range(own_count)]
     near = []
     for k in range(own_count):
         first = pl.multiple_of((places[k] // tile) * tile, tile)
         near.append(pltpu.make_async_copy(queries_hbm.at[pl.ds(first, tile)], near_ref.at[pl.ds(k * tile, tile)], near_sems.at[k]))
-    for copy in copies + near:
-        copy.start()
+        near[-1].start()
     lane = lax.broadcasted_iota(jnp.int32, (1, LANES), 1)
 
     def one_hot(places, size):
@@ -179,22 +197,28 @@
     place = jnp.full((2 * own_count, LANES), -1, jnp.int32)
     for k in range(own_count):
         place = jnp.where(row == k, k * tile + places[k] % tile, place)
-    copies[0].wait()
+    kept_copy.wait()
     offset = (kept_ref[...] - start).astype(jnp.float32)
     offset = jnp.transpose(jnp.broadcast_to(offset, (LANES, offset.shape[1])))
     chosen = one_hot(offset, slab_len)
+    for copy in copies:
+        copy.wait()
+    picked = jnp.dot(chosen, keys_ref[...], preferred_element_type=jnp.float32)
+    picked = picked.reshape(peers, -1, LANES)
     for copy in near:
         copy.wait()
     own = jnp.dot(one_hot(place.astype(jnp.float32), own_count * tile), near_ref[...], preferred_element_type=jnp.float32)
-    own = jnp.broadcast_to(own[None, :own_count], (peers, own_count, LANES))
-    for copy in copies[1:]:
+    half = peers // 2
+    own = jnp.broadcast_to(own[None, :own_count], (half, own_count, LANES))
+    moved = []
+    for k in range(2):
+        out_ref[k * half : (k + 1) * half] = jnp.concatenate([own, picked[k * half : (k + 1) * half]], axis=1).astype(jnp.bfloat16)
+        moved += sent_out(out_ref, out_hbm, out_sems.at[k], k * half, half)
+    for copy in moved:
         copy.wait()
-    picked = jnp.dot(chosen, keys_ref[...], preferred_element_type=jnp.float32)
-    picked = picked.reshape(peers, -1, LANES)
-    out_ref[...] = jnp.concatenate([own, picked], axis=1).astype(jnp.bfloat16)
-
-
-def attend_kernel(own_count, got_ref, keys_ref, values_ref, queries_ref, out_ref, word_ref, mark_ref):
+
+
+def attend_kernel(own_count, got_ref, keys_ref, values_ref, queries_ref, out_ref):
     peers = got_ref.shape[0]
     rows = peers * own_count
     inv_root = 1.0 / math.sqrt(keys_ref.shape[1])
@@ -202,24 +226,25 @@
     code = code_of(jnp.sum(got[:, own_count:], axis=0))
     queries_ref[...] = got[:, :own_count].reshape(rows, LANES).astype(jnp.bfloat16)
     block = rows // 2
+    stride = own_count + 1
     for at in range(0, rows, block):
         scores = lax.dot_general(
             queries_ref[at : at + block], keys_ref[...], (BY_COLUMN, ((), ())), preferred_element_type=jnp.float32
-        ) * inv_root
+        )
         peak = jnp.max(scores, axis=1, keepdims=True)
-        probs = jnp.exp(scores - peak).astype(jnp.bfloat16)
+        probs = jnp.exp2((scores - peak) * (inv_root * math.log2(math.e))).astype(jnp.bfloat16)
+        peak = peak * inv_root
         total = jnp.sum(probs.astype(jnp.float32), axis=1, keepdims=True)
-        mean = jnp.dot(probs, values_ref[...], preferred_element_type=jnp.float32) / total
-        whole, power = scaled(mean)
-        words = packed(whole.reshape(block // own_count, own_count, LANES), code[None])
-        word_ref[at : at + block] = words.reshape(block, LANES)
+        whole, power = scaled(jnp.dot(probs, values_ref[...], preferred_element_type=jnp.float32) / total)
         peak_mark = jnp.round(peak * PEAK_UNIT)
         share_mark = jnp.round((jnp.log(total) + (peak - peak_mark / PEAK_UNIT)) * SHARE_UNIT)
         marks = in_lanes((peak_mark, share_mark, power), own_count)
-        mark_ref[at // own_count : (at + block) // own_count] = marks.astype(jnp.int32)
-    for k in range(own_count):
-        out_ref[pl.ds(k, peers, stride=own_count + 1)] = every(word_ref, k, own_count)
-    out_ref[pl.ds(own_count, peers, stride=own_count + 1)] = mark_ref[...]
+        count = block // own_count
+        first = at // own_count * stride
+        for k in range(count):
+            words = packed(whole[k * own_count : (k + 1) * own_count], code)
+            out_ref[first + k * stride : first + k * stride + own_count] = words
+        out_ref[pl.ds(first + own_count, count, stride=stride)] = marks.astype(jnp.int32)
 
 
 def merge_kernel(words_ref, ref_out_ref, out_ref):
@@ -247,11 +272,11 @@
     words = packed(whole[:half], whole[half:])
     words = jnp.concatenate([words, in_lanes((power,), own_count).astype(jnp.int32)], axis=0)
     peers = out_ref.shape[0] // (half + 1)
-    for k in range(half + 1):
-        out_ref[pl.ds(k, peers, stride=half + 1)] = jnp.broadcast_to(words[k : k + 1], (peers, LANES))
-
-
-def finish_kernel(own_count, words_ref, high_ref, low_ref, out_ref, rows_ref):
+    for k in range(peers):
+        out_ref[k * (half + 1) : (k + 1) * (half + 1)] = words
+
+
+def finish_kernel(own_count, words_ref, high_ref, low_ref, out_hbm, out_ref, rows_ref, sems):
     half = own_count // 2
     peers = words_ref.shape[0] // (half + 1)
     scales = power_of_two(every(words_ref, half, half + 1).astype(jnp.float32)[:, :own_count]) * (1.0 / FULL)
@@ -259,7 +284,18 @@
         words = every(words_ref, k % half, half + 1)
         whole = high_of(words) if k < half else low_of(words)
         rows_ref[pl.ds(k, peers, stride=own_count)] = whole.astype(jnp.float32) * scales[:, k : k + 1]
-    out_ref[...] = product((high_ref[...], low_ref[...]), in_two(rows_ref[...]), ROWS)
+    high, low = in_two(rows_ref[...])
+    both = jnp.concatenate([high, low], axis=1)
+    size = out_ref.shape[0] // 2
+    moved = []
+    for part in range(2):
+        at = part * size
+        sums = jnp.dot(high_ref[at : at + size], both, preferred_element_type=jnp.float32)
+        rest = jnp.dot(low_ref[at : at + size], high, preferred_element_type=jnp.float32)
+        out_ref[at : at + size] = sums[:, :LANES] + (sums[:, LANES:] + rest)
+        moved += sent_out(out_ref, out_hbm, sems.at[part], at, size)
+    for copy in moved:
+        copy.wait()
 
 
 def per_device(keys, values, queries, query_positions, kept_index, ridge_level):
@@ -276,22 +312,25 @@
     whole = pltpu.CompilerParams(vmem_limit_bytes=60 * 2**20)
     small = pltpu.CompilerParams(vmem_limit_bytes=8 * 2**20)
     f32, bf16, i32 = jnp.float32, jnp.bfloat16, jnp.int32
-    slab_start = (lax.axis_index(SEQ) * slab_len).astype(i32).reshape(1)
     sent = pl.pallas_call(
         pick_kernel,
         out_shape=jax.ShapeDtypeStruct((peers, own_count + own_kept, head_dim), bf16),
-        in_specs=[smem, smem, hbm, hbm, hbm],
-        out_specs=vmem,
+        in_specs=[hbm] * 4,
+        out_specs=hbm,
         scratch_shapes=[
+            pltpu.SMEM((own_count,), i32),
             pltpu.VMEM((1, kept_count), i32),
             pltpu.VMEM((slab_len, head_dim), bf16),
             pltpu.VMEM((own_count * TILE, head_dim), bf16),
-            pltpu.SemaphoreType.DMA((KEY_PARTS + 1,)),
+            pltpu.VMEM((peers, own_count + own_kept, head_dim), bf16),
+            pltpu.SemaphoreType.DMA((2,)),
+            pltpu.SemaphoreType.DMA((KEY_PARTS,)),
             pltpu.SemaphoreType.DMA((own_count,)),
+            pltpu.SemaphoreType.DMA((2, 2)),
         ],
         compiler_params=whole,
         name="pick",
-    )(slab_start, query_positions, kept_index[None], keys, queries)
+    )(query_positions, kept_index[None], keys, queries)
     got = swap(sent)
     all_queries, words = pl.pallas_call(
         functools.partial(attend_kernel, own_count),
@@ -301,7 +340,6 @@
         ],
         in_specs=[vmem] * 3,
         out_specs=[vmem] * 2,
-        scratch_shapes=[pltpu.VMEM((rows, head_dim), i32), pltpu.VMEM((peers, LANES), i32)],
         compiler_params=roomy,
         name="attend",
     )(got, keys, values)
@@ -339,8 +377,12 @@
         functools.partial(finish_kernel, own_count),
         out_shape=jax.ShapeDtypeStruct((kept_count, head_dim), f32),
         in_specs=[vmem] * 3,
-        out_specs=vmem,
-        scratch_shapes=[pltpu.VMEM((rows, head_dim), f32)],
+        out_specs=hbm,
+        scratch_shapes=[
+            pltpu.VMEM((kept_count, head_dim), f32),
+            pltpu.VMEM((rows, head_dim), f32),
+            pltpu.SemaphoreType.DMA((2, 2)),
+        ],
         compiler_params=roomy,
         name="finish",
     )(means, high, low)

time: 101 us -> 99.7 us (0.987)
  waiting for transfers between devices: 24.2 us -> 22.4 us
    pallas_call x1, Pallas kernels: 12.8 us -> 14.6 us  [per_device(): pl.pallas_call(functools.partial(solve_kernel, own_count), out_shape=[jax...]
    all_to_all x2, waiting for transfers between devices: 24.2 us -> 22.4 us  [swap(): return lax.all_to_all(blocks, SEQ, 0, 0, tiled=True)]
  transfers between devices with their start and end apart: 2 -> 2, of which waited for: 2 -> 2; matrix products, arithmetic and copies ran while one was open for 0% -> 0% of each run, Pallas kernels for 13% -> 15%
where the time goes in v4:
time: 99.7 us; the launch traced here: 99.4 us
  blocking collectives  39.7 us (40%)
  Pallas kernels  22.8 us (23%)
  waiting for transfers between devices  22.4 us (22%)
  starting transfers between devices  13 us (13%)
  between operations  1.49 us (1%)
    all_to_all x1, blocking collectives, swap(): return lax.all_to_all(blocks, SEQ, 0, 0, tiled=True)  39.7 us
    all_to_all x2, waiting for transfers between devices, swap(): return lax.all_to_all(blocks, SEQ, 0, 0, tiled=True)  22.4 us
    pallas_call x1, Pallas kernels, per_device(): pl.pallas_call(functools.partial(solve_kernel, own_count), out_shape=[jax...  14.6 us
    all_to_all x2, starting transfers between devices, swap(): return lax.all_to_all(blocks, SEQ, 0, 0, tiled=True)  13 us
    pallas_call x1, Pallas kernels, per_device(): pl.pallas_call(functools.partial(attend_kernel, own_count), out_shape=[ja...  2.96 us
    pallas_call x1, Pallas kernels, per_device(): pl.pallas_call(pick_kernel, out_shape=jax.ShapeDtypeStruct((peers, own_co...  2.88 us
  transfers between devices with their start and end apart: 2, of which 2 were waited for; matrix products, arithmetic and copies ran while one was open for 0% of the time, Pallas kernels for 15%

profile of v4, /device:TPU:24, one launch (start us, length us, event | category | flops | bytes accessed | tf_op | source)
XLA Modules:
  0.0 99.4 jit_solution(11375303381627114088)
XLA Ops:
  0.6 0.0 copy-start.1
  0.6 2.9 %pick.1 = bf16[64,16,128]{2,1,0:T(8,128)(2,1)} custom-call(s32[8]{0:T(128)} %positions_hbm.1, s32[1,512]{1,0:T(1,128)} %bitcast.8, bf16[2048,128]{1,0:T(8,128)(2,1)} %keys_ref.1, bf16[2048,128]{1,0:T(8,128)(2,1)} %queries_hbm.1), custom_call_target="tpu_custom_call" | custom-call | tf_op jit(solution)/shard_map/pick/pallas_call | solution.py:315
  3.5 0.0 copy-start
  3.5 39.7 %all_to_all.15.got_ref = bf16[64,16,128]{2,1,0:T(8,128)(2,1)S(1)} all-to-all(bf16[64,16,128]{2,1,0:T(8,128)(2,1)} %pick.1), channel_id=1, replica_groups=mesh['head'=8,'seq'=64] {'seq'}, dimensions={0} | all-to-all | bytes 524288 | tf_op jit(solution)/shard_map/all_to_all | solution.py:22
  43.2 0.0 copy-done.1
  43.2 0.0 copy-done
  43.2 3.0 %attend.1 = (bf16[512,128]{1,0:T(8,128)(2,1)S(1)}, s32[576,128]{1,0:T(8,128)}) custom-call(bf16[64,16,128]{2,1,0:T(8,128)(2,1)S(1)} %all_to_all.15.got_ref, bf16[2048,128]{1,0:T(8,128)(2,1)S(1)} %copy-done, bf16[2048,128]{1,0:T(8,128)(2,1)S(1)} %copy-done.1), custom_call_target="tpu_custom_call" | custom-call | tf_op jit(solution)/shard_map/attend/pallas_call | solution.py:335
  46.2 6.5 %all-to-all-start.1 = ((s32[64,9,1,128]{3,2,1,0:T(1,128)}), s32[64,9,1,128]{3,2,1,0:T(1,128)S(1)}, u32[]{:S(2)}, u32[]{:S(2)}) async-start(s32[64,9,1,128]{3,2,1,0:T(1,128)} %bitcast.1), calls=%async_computation.1 | async-start | bytes 589824 | tf_op jit(solution)/shard_map/all_to_all | solution.py:22
  53.3 20.9 %all-to-all-done.1 = s32[64,9,1,128]{3,2,1,0:T(1,128)S(1)} async-done(((s32[64,9,1,128]{3,2,1,0:T(1,128)}), s32[64,9,1,128]{3,2,1,0:T(1,128)S(1)}, u32[]{:S(2)}, u32[]{:S(2)}) %all-to-all-start.1) | async-done | bytes 294944 | tf_op jit(solution)/shard_map/all_to_all | solution.py:22
  74.2 1.1 %merge.1 = (f32[8,128]{1,0:T(8,128)}, s32[320,128]{1,0:T(8,128)}) custom-call(s32[576,128]{1,0:T(8,128)S(1)} %bitcast.5), custom_call_target="tpu_custom_call" | custom-call | tf_op jit(solution)/shard_map/merge/pallas_call | solution.py:347
  75.3 6.5 %all-to-all-start.2 = ((s32[64,5,1,128]{3,2,1,0:T(1,128)}), s32[64,5,1,128]{3,2,1,0:T(1,128)S(1)}, u32[]{:S(2)}, u32[]{:S(2)}) async-start(s32[64,5,1,128]{3,2,1,0:T(1,128)} %bitcast.3), calls=%async_computation.2 | async-start | bytes 327680 | tf_op jit(solution)/shard_map/all_to_all | solution.py:22
  81.8 14.6 %solve.1 = (bf16[512,512]{1,0:T(8,128)(2,1)S(1)}, bf16[512,512]{1,0:T(8,128)(2,1)S(1)}) custom-call(s32[1]{0:T(128)S(6)} %copy.10.level_ref, bf16[512,128]{1,0:T(8,128)(2,1)S(1)} %get-tuple-element.10.queries_ref, s32[576,128]{1,0:T(8,128)S(1)} %bitcast.6), custom_call_target="tpu_custom_call" | custom-call | flops 12000000000 | bytes 2097152 | tf_op jit(solution)/shard_map/solve/pallas_call | solution.py:360
  96.5 1.5 %all-to-all-done.2 = s32[64,5,1,128]{3,2,1,0:T(1,128)S(1)} async-done(((s32[64,5,1,128]{3,2,1,0:T(1,128)}), s32[64,5,1,128]{3,2,1,0:T(1,128)S(1)}, u32[]{:S(2)}, u32[]{:S(2)}) %all-to-all-start.2) | async-done | bytes 163872 | tf_op jit(solution)/shard_map/all_to_all | solution.py:22
  97.9 1.3 %finish.1 = f32[512,128]{1,0:T(8,128)} custom-call(s32[320,128]{1,0:T(8,128)S(1)} %bitcast.7, bf16[512,512]{1,0:T(8,128)(2,1)S(1)} %get-tuple-element.11.high_ref, bf16[512,512]{1,0:T(8,128)(2,1)S(1)} %get-tuple-element.12.low_ref), custom_call_target="tpu_custom_call" | custom-call | tf_op jit(solution)/shard_map/finish/pallas_call | solution.py:376
Async XLA Ops:
  0.6 42.6 %copy-start.1 = (bf16[2048,128]{1,0:T(8,128)(2,1)S(1)}, bf16[2048,128]{1,0:T(8,128)(2,1)}, u32[]{:S(2)}) copy-start(bf16[2048,128]{1,0:T(8,128)(2,1)} %values_ref.1) | copy-start | bytes 1572868
  3.5 39.7 %copy-start = (bf16[2048,128]{1,0:T(8,128)(2,1)S(1)}, bf16[2048,128]{1,0:T(8,128)(2,1)}, u32[]{:S(2)}) copy-start(bf16[2048,128]{1,0:T(8,128)(2,1)} %keys_ref.1) | copy-start | bytes 1572868
  46.2 28.0 %all-to-all-start.1 = ((s32[64,9,1,128]{3,2,1,0:T(1,128)}), s32[64,9,1,128]{3,2,1,0:T(1,128)S(1)}, u32[]{:S(2)}, u32[]{:S(2)}) async-start(s32[64,9,1,128]{3,2,1,0:T(1,128)} %bitcast.1), calls=%async_computation.1 | async-start | bytes 589824 | tf_op jit(solution)/shard_map/all_to_all | solution.py:22
  75.3 22.7 %all-to-all-start.2 = ((s32[64,5,1,128]{3,2,1,0:T(1,128)}), s32[64,5,1,128]{3,2,1,0:T(1,128)S(1)}, u32[]{:S(2)}, u32[]{:S(2)}) async-start(s32[64,5,1,128]{3,2,1,0:T(1,128)} %bitcast.3), calls=%async_computation.2 | async-start | bytes 327680 | tf_op jit(solution)/shard_map/all_to_all | solution.py:22

commit v5 on v4

--- a/solution.py
+++ b/solution.py
@@ -100,7 +100,7 @@
 BY_COLUMN = ((1,), (1,))
 
 
-def solve_kernel(own_count, level_ref, queries_ref, words_ref, high_ref, low_ref, kept_ref, system_ref, weights_ref, inverse_ref, rest_ref):
+def solve_kernel(own_count, ridge_ref, queries_ref, words_ref, high_ref, low_ref, kept_ref, system_ref, weights_ref, inverse_ref, rest_ref):
     size = system_ref.shape[0]
     inv_root = 1.0 / math.sqrt(queries_ref.shape[1])
     for k in range(own_count):
@@ -114,7 +114,7 @@
     weights_ref[...] = weights
     parts = in_two(weights)
     gram = product(parts, parts, BY_ROW)
-    ridge = level_ref[0].astype(jnp.float32) * 0.01
+    ridge = jnp.max(ridge_ref[...])
     bound = jnp.max(jnp.sum(weights, axis=0, keepdims=True), axis=1, keepdims=True) * 1.0001
     row = lax.broadcasted_iota(jnp.int32, (size, size), 0)
     column = lax.broadcasted_iota(jnp.int32, (size, size), 1)
@@ -157,8 +157,8 @@
 
 
 def pick_kernel(
-    positions_hbm, kept_hbm, keys_hbm, queries_hbm, out_hbm,
-    positions_ref, kept_ref, keys_ref, near_ref, out_ref, first_sems, sems, near_sems, out_sems,
+    level_hbm, positions_hbm, kept_hbm, keys_hbm, queries_hbm, out_hbm, ridge_hbm,
+    level_ref, positions_ref, kept_ref, keys_ref, near_ref, out_ref, ridge_ref, first_sems, sems, near_sems, out_sems, ridge_sem,
 ):
     slab_len = keys_ref.shape[0]
     peers = out_ref.shape[0]
@@ -168,8 +168,10 @@
     rest = keys_ref.shape[0] // KEY_PARTS
     positions_copy = pltpu.make_async_copy(positions_hbm, positions_ref, first_sems.at[0])
     kept_copy = pltpu.make_async_copy(kept_hbm, kept_ref, first_sems.at[1])
+    level_copy = pltpu.make_async_copy(level_hbm, level_ref, first_sems.at[2])
     positions_copy.start()
     kept_copy.start()
+    level_copy.start()
     copies = []
     for k in range(KEY_PARTS):
         part = pl.ds(k * rest, rest)
@@ -201,6 +203,10 @@
     offset = (kept_ref[...] - start).astype(jnp.float32)
     offset = jnp.transpose(jnp.broadcast_to(offset, (LANES, offset.shape[1])))
     chosen = one_hot(offset, slab_len)
+    level_copy.wait()
+    ridge_ref[...] = jnp.full(ridge_ref.shape, level_ref[0].astype(jnp.float32) * 0.01)
+    ridge_copy = pltpu.make_async_copy(ridge_ref, ridge_hbm, ridge_sem)
+    ridge_copy.start()
     for copy in copies:
         copy.wait()
     picked = jnp.dot(chosen, keys_ref[...], preferred_element_type=jnp.float32)
@@ -214,6 +220,7 @@
     for k in range(2):
         out_ref[k * half : (k + 1) * half] = jnp.concatenate([own, picked[k * half : (k + 1) * half]], axis=1).astype(jnp.bfloat16)
         moved += sent_out(out_ref, out_hbm, out_sems.at[k], k * half, half)
+    ridge_copy.wait()
     for copy in moved:
         copy.wait()
 
@@ -306,31 +313,36 @@
     own_kept = kept_count // peers
     rows = peers * own_count
     vmem = pl.BlockSpec(memory_space=pltpu.VMEM)
-    smem = pl.BlockSpec(memory_space=pltpu.SMEM)
     hbm = pl.BlockSpec(memory_space=pltpu.HBM)
     roomy = pltpu.CompilerParams(vmem_limit_bytes=24 * 2**20)
     whole = pltpu.CompilerParams(vmem_limit_bytes=60 * 2**20)
     small = pltpu.CompilerParams(vmem_limit_bytes=8 * 2**20)
     f32, bf16, i32 = jnp.float32, jnp.bfloat16, jnp.int32
-    sent = pl.pallas_call(
+    sent, ridge = pl.pallas_call(
         pick_kernel,
-        out_shape=jax.ShapeDtypeStruct((peers, own_count + own_kept, head_dim), bf16),
-        in_specs=[hbm] * 4,
-        out_specs=hbm,
+        out_shape=[
+            jax.ShapeDtypeStruct((peers, own_count + own_kept, head_dim), bf16),
+            jax.ShapeDtypeStruct((8, LANES), f32),
+        ],
+        in_specs=[hbm] * 5,
+        out_specs=[hbm] * 2,
         scratch_shapes=[
+            pltpu.SMEM((1,), i32),
             pltpu.SMEM((own_count,), i32),
             pltpu.VMEM((1, kept_count), i32),
             pltpu.VMEM((slab_len, head_dim), bf16),
             pltpu.VMEM((own_count * TILE, head_dim), bf16),
             pltpu.VMEM((peers, own_count + own_kept, head_dim), bf16),
-            pltpu.SemaphoreType.DMA((2,)),
+            pltpu.VMEM((8, LANES), f32),
+            pltpu.SemaphoreType.DMA((3,)),
             pltpu.SemaphoreType.DMA((KEY_PARTS,)),
             pltpu.SemaphoreType.DMA((own_count,)),
             pltpu.SemaphoreType.DMA((2, 2)),
+            pltpu.SemaphoreType.DMA,
         ],
         compiler_params=whole,
         name="pick",
-    )(query_positions, kept_index[None], keys, queries)
+    )(ridge_level, query_positions, kept_index[None], keys, queries)
     got = swap(sent)
     all_queries, words = pl.pallas_call(
         functools.partial(attend_kernel, own_count),
@@ -360,7 +372,7 @@
     high, low = pl.pallas_call(
         functools.partial(solve_kernel, own_count),
         out_shape=[jax.ShapeDtypeStruct((kept_count, rows), bf16)] * 2,
-        in_specs=[smem, vmem, vmem],
+        in_specs=[vmem] * 3,
         out_specs=[vmem] * 2,
         scratch_shapes=[
             pltpu.VMEM((kept_count, head_dim), f32),
@@ -372,7 +384,7 @@
         compiler_params=roomy,
         cost_estimate=pl.CostEstimate(flops=12 * 10**9, bytes_accessed=2 * 2**20, transcendentals=2**18),
         name="solve",
-    )(ridge_level, all_queries, words)
+    )(ridge, all_queries, words)
     matched_values = pl.pallas_call(
         functools.partial(finish_kernel, own_count),
         out_shape=jax.ShapeDtypeStruct((kept_count, head_dim), f32),

time: 99.7 us -> 99.6 us (level)
  blocking collectives: 39.7 us -> 67.4 us
  waiting for transfers between devices: 22.4 us -> 3.31 us
  starting transfers between devices: 13 us -> 6.72 us
  Pallas kernels: 22.8 us -> 20.3 us
    all_to_all x1 -> x2, blocking collectives: 39.7 us -> 67.4 us  [swap(): return lax.all_to_all(blocks, SEQ, 0, 0, tiled=True)]
    all_to_all x2 -> x1, waiting for transfers between devices: 22.4 us -> 3.31 us  [swap(): return lax.all_to_all(blocks, SEQ, 0, 0, tiled=True)]
    all_to_all x2 -> x1, starting transfers between devices: 13 us -> 6.72 us  [swap(): return lax.all_to_all(blocks, SEQ, 0, 0, tiled=True)]
    pallas_call x1, Pallas kernels: 14.6 us -> 12.8 us  [per_device(): pl.pallas_call(functools.partial(solve_kernel, own_count), out_shape=[jax...]
  transfers between devices with their start and end apart: 2 -> 1, of which waited for: 2 -> 1; matrix products, arithmetic and copies ran while one was open for 0% -> 0% of each run, Pallas kernels for 15% -> 13%
where the time goes in v5:
time: 99.6 us; the launch traced here: 99.2 us
  blocking collectives  67.4 us (68%)
  Pallas kernels  20.3 us (20%)
  starting transfers between devices  6.72 us (7%)
  waiting for transfers between devices  3.31 us (3%)
  between operations  1.49 us (1%)
    all_to_all x2, blocking collectives, swap(): return lax.all_to_all(blocks, SEQ, 0, 0, tiled=True)  67.4 us
    pallas_call x1, Pallas kernels, per_device(): pl.pallas_call(functools.partial(solve_kernel, own_count), out_shape=[jax...  12.8 us
    all_to_all x1, starting transfers between devices, swap(): return lax.all_to_all(blocks, SEQ, 0, 0, tiled=True)  6.72 us
    all_to_all x1, waiting for transfers between devices, swap(): return lax.all_to_all(blocks, SEQ, 0, 0, tiled=True)  3.31 us
    pallas_call x1, Pallas kernels, per_device(): pl.pallas_call(pick_kernel, out_shape=[jax.ShapeDtypeStruct((peers, own_c...  2.9 us
    pallas_call x1, Pallas kernels, per_device(): pl.pallas_call(functools.partial(attend_kernel, own_count), out_shape=[ja...  2.24 us
  transfers between devices with their start and end apart: 1, of which 1 were waited for; matrix products, arithmetic and copies ran while one was open for 0% of the time, Pallas kernels for 13%

profile of v5, /device:TPU:24, one launch (start us, length us, event | category | flops | bytes accessed | tf_op | source)
XLA Modules:
  0.0 99.2 jit_solution(11417880249455683434)
XLA Ops:
  1.3 0.0 copy-start.1
  1.3 2.9 %pick.1 = (bf16[64,16,128]{2,1,0:T(8,128)(2,1)}, f32[8,128]{1,0:T(8,128)}) custom-call(s32[1]{0:T(128)S(6)} %copy.10.level_hbm, s32[8]{0:T(128)} %positions_hbm.1, s32[1,512]{1,0:T(1,128)} %bitcast.9, bf16[2048,128]{1,0:T(8,128)(2,1)} %keys_ref.1, bf16[2048,128]{1,0:T(8,128)(2,1)} %queries_hbm.1), custom_call_target="tpu_custom_call" | custom-call | tf_op jit(solution)/shard_map/pick/pallas_call | solution.py:321
  4.2 0.0 copy-start
  4.2 39.7 %all_to_all.15.got_ref = bf16[64,16,128]{2,1,0:T(8,128)(2,1)S(1)} all-to-all(bf16[64,16,128]{2,1,0:T(8,128)(2,1)} %get-tuple-element.10), channel_id=1, replica_groups=mesh['head'=8,'seq'=64] {'seq'}, dimensions={0} | all-to-all | bytes 524288 | tf_op jit(solution)/shard_map/all_to_all | solution.py:22
  43.9 0.0 copy-done.1
  43.9 0.0 copy-done
  43.9 2.2 %attend.1 = (bf16[512,128]{1,0:T(8,128)(2,1)S(1)}, s32[576,128]{1,0:T(8,128)S(1)}) custom-call(bf16[64,16,128]{2,1,0:T(8,128)(2,1)S(1)} %all_to_all.15.got_ref, bf16[2048,128]{1,0:T(8,128)(2,1)S(1)} %copy-done, bf16[2048,128]{1,0:T(8,128)(2,1)S(1)} %copy-done.1), custom_call_target="tpu_custom_call" | custom-call | tf_op jit(solution)/shard_map/attend/pallas_call | solution.py:347
  46.1 27.7 %all_to_all.16 = s32[64,9,1,128]{3,2,1,0:T(1,128)S(1)} all-to-all(s32[64,9,1,128]{3,2,1,0:T(1,128)S(1)} %bitcast.8), channel_id=1, replica_groups=mesh['head'=8,'seq'=64] {'seq'}, dimensions={0} | all-to-all | bytes 589824 | tf_op jit(solution)/shard_map/all_to_all | solution.py:22
  73.9 1.1 %merge.1 = (f32[8,128]{1,0:T(8,128)}, s32[320,128]{1,0:T(8,128)}) custom-call(s32[576,128]{1,0:T(8,128)S(1)} %bitcast.5), custom_call_target="tpu_custom_call" | custom-call | tf_op jit(solution)/shard_map/merge/pallas_call | solution.py:359
  75.0 0.0 copy-start.2
  75.0 6.7 %all-to-all-start.2 = ((s32[64,5,1,128]{3,2,1,0:T(1,128)}), s32[64,5,1,128]{3,2,1,0:T(1,128)S(1)}, u32[]{:S(2)}, u32[]{:S(2)}) async-start(s32[64,5,1,128]{3,2,1,0:T(1,128)} %bitcast.3), calls=%async_computation.2 | async-start | bytes 327680 | tf_op jit(solution)/shard_map/all_to_all | solution.py:22
  81.7 0.0 copy-done.2
  81.7 12.8 %solve.1 = (bf16[512,512]{1,0:T(8,128)(2,1)S(1)}, bf16[512,512]{1,0:T(8,128)(2,1)S(1)}) custom-call(f32[8,128]{1,0:T(8,128)S(1)} %copy-done.2, bf16[512,128]{1,0:T(8,128)(2,1)S(1)} %get-tuple-element.14.queries_ref, s32[576,128]{1,0:T(8,128)S(1)} %bitcast.6), custom_call_target="tpu_custom_call" | custom-call | flops 12000000000 | bytes 2097152 | tf_op jit(solution)/shard_map/solve/pallas_call | solution.py:372
  94.5 3.3 %all-to-all-done.2 = s32[64,5,1,128]{3,2,1,0:T(1,128)S(1)} async-done(((s32[64,5,1,128]{3,2,1,0:T(1,128)}), s32[64,5,1,128]{3,2,1,0:T(1,128)S(1)}, u32[]{:S(2)}, u32[]{:S(2)}) %all-to-all-start.2) | async-done | bytes 163872 | tf_op jit(solution)/shard_map/all_to_all | solution.py:22
  97.8 1.3 %finish.1 = f32[512,128]{1,0:T(8,128)} custom-call(s32[320,128]{1,0:T(8,128)S(1)} %bitcast.7, bf16[512,512]{1,0:T(8,128)(2,1)S(1)} %get-tuple-element.15.high_ref, bf16[512,512]{1,0:T(8,128)(2,1)S(1)} %get-tuple-element.16.low_ref), custom_call_target="tpu_custom_call" | custom-call | tf_op jit(solution)/shard_map/finish/pallas_call | solution.py:388
Async XLA Ops:
  1.3 42.6 %copy-start.1 = (bf16[2048,128]{1,0:T(8,128)(2,1)S(1)}, bf16[2048,128]{1,0:T(8,128)(2,1)}, u32[]{:S(2)}) copy-start(bf16[2048,128]{1,0:T(8,128)(2,1)} %values_ref.1) | copy-start | bytes 1572868
  4.2 39.7 %copy-start = (bf16[2048,128]{1,0:T(8,128)(2,1)S(1)}, bf16[2048,128]{1,0:T(8,128)(2,1)}, u32[]{:S(2)}) copy-start(bf16[2048,128]{1,0:T(8,128)(2,1)} %keys_ref.1) | copy-start | bytes 1572868
  75.0 6.7 %copy-start.2 = (f32[8,128]{1,0:T(8,128)S(1)}, f32[8,128]{1,0:T(8,128)}, u32[]{:S(2)}) copy-start(f32[8,128]{1,0:T(8,128)} %get-tuple-element.13.ridge_ref) | copy-start | bytes 12292
  75.0 22.9 %all-to-all-start.2 = ((s32[64,5,1,128]{3,2,1,0:T(1,128)}), s32[64,5,1,128]{3,2,1,0:T(1,128)S(1)}, u32[]{:S(2)}, u32[]{:S(2)}) async-start(s32[64,5,1,128]{3,2,1,0:T(1,128)} %bitcast.3), calls=%async_computation.2 | async-start | bytes 327680 | tf_op jit(solution)/shard_map/all_to_all | solution.py:22
